TPU v7x, 32 devices: a whole 2x2x4 slice. The times are simulated.
32 devices in a mesh: row: 4 (over z), col: 8 (over y, x, core).
Axes of the slice: x: 2, y: 2, z: 4, core: 2. Of those that a mesh axis runs over, the one named last changes fastest.
Arguments:
- front: float32 [16384, 16384], P('row', 'col')
- tiles: float32 [4096, 128, 128], P(('row', 'col')), may hold values from -0.375 to 0.375
- tile_block: int32 [2, 4096], replicated, may hold values from 0 to 127, as said below
- valid_rows: int32 [4096], P(('row', 'col')), may hold values from 64 to 128
Outputs:
- factored: float32 [16384, 16384], P('row', 'col')
Inputs may be any that keep to these rules, and one draw needn't show every extreme that they name: tile_block[0, t] and tile_block[1, t] give the block row and block column, in blocks of 128, that tile t is added to. The 128 tiles of each device (tiles laid in order over row+col) go to blocks held by exactly 16 different devices, 8 tiles to each.
All inputs are finite; a program needn't handle non-finite values.
Results may differ from a plain program's by a relative error of at most 0.0001.
Values sent between devices are 32-bit elements; how exact they have to be, the bound alone decides.
No kernel may reach another device: no remote copies, remote signals or barrier semaphores. Data moves between devices by JAX's collectives and lax.ppermute only.
A program may use at most 192 MiB of HBM per device.

v0:
```python
import functools

import jax
import jax.numpy as jnp
from jax import lax
from jax.experimental import pallas as pl
from jax.experimental.pallas import tpu as pltpu
from jax.sharding import PartitionSpec as P

NB = 128
PANELS = 2
TOTAL = NB * PANELS
MIB = 1 << 20
UNIT = 8


precise = lax.Precision.HIGHEST


def dot_nt(a, b, precision=precise):
    return lax.dot_general(
        a, b, (((1,), (1,)), ((), ())), precision=precision, preferred_element_type=jnp.float32
    )


def pack_kernel(slot_ref, valid_ref, tiles_ref, out_ref, buf, sem_in, sem_out):
    count, side = tiles_ref.shape[0], tiles_ref.shape[1]

    def fetch(t):
        return pltpu.make_async_copy(tiles_ref.at[t], buf.at[t], sem_in.at[t])

    def store(t):
        return pltpu.make_async_copy(buf.at[t], out_ref.at[jnp.maximum(slot_ref[t], 0)], sem_out.at[t])

    def each(act):
        @pl.loop(0, count)
        def _(t):
            @pl.when(slot_ref[t] >= 0)
            def _():
                act(t)

    def mask(t):
        fetch(t).wait()
        rows = lax.broadcasted_iota(jnp.int32, (side, side), 0)
        buf[t] = jnp.where(rows < valid_ref[t], buf[t], 0.0)
        store(t).start()

    each(lambda t: fetch(t).start())
    each(mask)
    each(lambda t: store(t).wait())


def pack(tiles, slots, valid, n_slots):
    count, side = tiles.shape[0], tiles.shape[1]
    smem = pl.BlockSpec(memory_space=pltpu.SMEM)
    return pl.pallas_call(
        pack_kernel,
        out_shape=jax.ShapeDtypeStruct((n_slots, side, side), jnp.float32),
        in_specs=[smem, smem, pl.BlockSpec(memory_space=pl.ANY)],
        out_specs=pl.BlockSpec(memory_space=pl.ANY),
        scratch_shapes=[
            pltpu.VMEM((count, side, side), jnp.float32),
            pltpu.SemaphoreType.DMA((count,)),
            pltpu.SemaphoreType.DMA((count,)),
        ],
        compiler_params=pltpu.CompilerParams(vmem_limit_bytes=24 * MIB),
    )(slots, valid, tiles)


def spread_kernel(
    width, stride, meta_ref, empty_ref, count_ref, tiles_ref, out_ref, code_ref, stage, sem
):
    count, units = tiles_ref.shape[0], tiles_ref.shape[1]
    devices, length = code_ref.shape

    @pl.loop(0, devices)
    def _(d):
        for k in range(length):
            code_ref[d, k] = -1

    @pl.loop(0, count)
    def _(i):
        tile, target, base = meta_ref[0, i], meta_ref[1, i], meta_ref[2, i]
        filled, code, valid = meta_ref[3, i], meta_ref[4, i], meta_ref[5, i]
        shape = tiles_ref.shape[1:]
        rows = lax.broadcasted_iota(jnp.int32, shape, 0) * shape[1]
        rows += lax.broadcasted_iota(jnp.int32, shape, 1)
        stage[target, pl.ds(base, units)] = jnp.where(rows < valid, tiles_ref[tile], 0.0)
        for u in range(units):
            code_ref[target, base + u] = jnp.where(u < filled, code + u * stride, -1)

    for half in range(2):
        first = 0 if half == 0 else count_ref[0]
        last = count_ref[0] if half == 0 else count
        free = count_ref[1 + half]

        def each_tile(i, carry):
            target, base, filled = meta_ref[1, i], meta_ref[2, i], meta_ref[3, i]

            def each_unit(q, carry):
                at, depth = carry
                relay = empty_ref[half, at]
                place = jnp.minimum(depth, width - 1)
                stage[relay, place] = stage[target, q]
                code_ref[relay, place] = code_ref[target, q]
                wrap = at + 1 >= free
                return jnp.where(wrap, 0, at + 1), jnp.where(wrap, depth + 1, depth)

            return lax.fori_loop(jnp.maximum(base, width), base + filled, each_unit, carry)

        lax.fori_loop(first, last, each_tile, (jnp.int32(0), jnp.int32(0)))

    copy = pltpu.make_async_copy(stage.at[:, pl.ds(0, width)], out_ref, sem)
    copy.start()
    copy.wait()


def spread(tiles, meta, empties, counts, devices, width, length, stride):
    count, side = tiles.shape[0], tiles.shape[1]
    units = side // UNIT
    smem = pl.BlockSpec(memory_space=pltpu.SMEM)
    return pl.pallas_call(
        functools.partial(spread_kernel, width, stride),
        out_shape=[
            jax.ShapeDtypeStruct((devices, width, UNIT, side), jnp.float32),
            jax.ShapeDtypeStruct((devices, length), jnp.int32),
        ],
        in_specs=[smem, smem, smem, pl.BlockSpec(memory_space=pltpu.VMEM)],
        out_specs=[pl.BlockSpec(memory_space=pl.ANY), smem],
        scratch_shapes=[
            pltpu.VMEM((devices, length, UNIT, side), jnp.float32),
            pltpu.SemaphoreType.DMA,
        ],
        compiler_params=pltpu.CompilerParams(vmem_limit_bytes=40 * MIB),
    )(meta, empties, counts, tiles.reshape(count, units, UNIT, side))


def relay_kernel(slot_ref, arrived_ref, out_ref):
    devices, width = slot_ref.shape

    @pl.loop(0, devices)
    def _(s):
        def more(k):
            return (k < width) & (slot_ref[s, jnp.minimum(k, width - 1)] >= 0)

        def move(k):
            out_ref[slot_ref[s, k]] = arrived_ref[s, k]
            return k + 1

        lax.while_loop(more, move, jnp.int32(0))


def relay(slots, arrived, length):
    vmem = pl.BlockSpec(memory_space=pltpu.VMEM)
    return pl.pallas_call(
        relay_kernel,
        out_shape=jax.ShapeDtypeStruct((length,) + arrived.shape[2:], jnp.float32),
        in_specs=[pl.BlockSpec(memory_space=pltpu.SMEM), vmem],
        out_specs=vmem,
        compiler_params=pltpu.CompilerParams(vmem_limit_bytes=40 * MIB),
    )(slots, arrived)


def add_kernel(
    cols_blocks, block_ref, unit_ref, index_ref, count_ref, partial_ref, arrived_ref, out_ref, buf,
    group_start, sem_in, sem_out
):
    slots, side = buf.shape[0], buf.shape[1]
    unit = arrived_ref.shape[1]
    ahead = slots // 2
    count = count_ref[0]

    def listed(i, carry):
        groups, last = carry
        block = block_ref[i]
        fresh = block != last

        @pl.when(fresh)
        def _():
            group_start[groups] = i

        return jnp.where(fresh, groups + 1, groups), block

    groups, _ = lax.fori_loop(0, count, listed, (jnp.int32(0), jnp.int32(-1)))
    group_start[groups] = count

    def window(g):
        block = block_ref[group_start[g]]
        rows = pl.ds(pl.multiple_of(block // cols_blocks * side, side), side)
        columns = pl.ds(pl.multiple_of(block % cols_blocks * side, side), side)
        return out_ref.at[rows, columns]

    def fetch(g):
        at = g % slots
        return pltpu.make_async_copy(window(g), buf.at[at], sem_in.at[at])

    def store(g):
        at = g % slots
        return pltpu.make_async_copy(buf.at[at], window(g), sem_out.at[at])

    @pl.loop(0, jnp.minimum(groups, ahead))
    def _(g):
        fetch(g).start()

    @pl.loop(0, groups)
    def _(g):
        @pl.when(g + ahead < groups)
        def _():
            @pl.when(g >= ahead)
            def _():
                store(g - ahead).wait()

            fetch(g + ahead).start()

        fetch(g).wait()

        @pl.loop(group_start[g], group_start[g + 1])
        def _(i):
            rows = pl.ds(pl.multiple_of(unit_ref[i] * unit, unit), unit)
            buf[g % slots, rows] += arrived_ref[index_ref[i]]

        store(g).start()

    @pl.loop(jnp.maximum(groups - slots, 0), groups)
    def _(g):
        store(g).wait()


def add_relayed(partial, arrived, listing, cols_blocks):
    row_len, col_len = partial.shape
    unit, side = arrived.shape[1:]
    smem = pl.BlockSpec(memory_space=pltpu.SMEM)
    hbm = pl.BlockSpec(memory_space=pl.ANY)
    return pl.pallas_call(
        functools.partial(add_kernel, cols_blocks),
        out_shape=jax.ShapeDtypeStruct((row_len, col_len), jnp.float32),
        in_specs=[smem, smem, smem, smem, hbm, pl.BlockSpec(memory_space=pltpu.VMEM)],
        out_specs=hbm,
        scratch_shapes=[
            pltpu.VMEM((16, side, side), jnp.float32),
            pltpu.SMEM((arrived.shape[0] + 1,), jnp.int32),
            pltpu.SemaphoreType.DMA((16,)),
            pltpu.SemaphoreType.DMA((16,)),
        ],
        input_output_aliases={4: 0},
        compiler_params=pltpu.CompilerParams(vmem_limit_bytes=24 * MIB),
    )(*listing, partial, arrived)


def panel_kernel(code_ref, first_ref, front_ref, arrived_ref, out_ref):
    side = arrived_ref.shape[1]

    @pl.when(first_ref[0] == 1)
    def _():
        out_ref[...] = front_ref[...]

    @pl.when(first_ref[0] == 0)
    def _():
        out_ref[...] = jnp.zeros_like(out_ref)

    @pl.loop(0, arrived_ref.shape[0])
    def _(k):
        code = code_ref[k]
        for part in range(PANELS):

            @pl.when((code >= 0) & (code % PANELS == part))
            def _():
                rows = pl.ds(pl.multiple_of(code // PANELS * side, side), side)
                out_ref[rows, part * side : (part + 1) * side] += arrived_ref[k]


def raw_panel(front, arrived, codes, first):
    row_len = front.shape[0]
    smem = pl.BlockSpec(memory_space=pltpu.SMEM)
    return pl.pallas_call(
        panel_kernel,
        grid=(1,),
        out_shape=jax.ShapeDtypeStruct((row_len, TOTAL), jnp.float32),
        in_specs=[
            smem,
            smem,
            pl.BlockSpec((row_len, TOTAL), lambda i: (0, 0)),
            pl.BlockSpec(arrived.shape, lambda i: (0, 0, 0)),
        ],
        out_specs=pl.BlockSpec((row_len, TOTAL), lambda i: (0, 0)),
        compiler_params=pltpu.CompilerParams(vmem_limit_bytes=40 * MIB),
    )(codes, first, front, arrived)


def split(value):
    high = value.astype(jnp.bfloat16)
    low = (value - high.astype(jnp.float32)).astype(jnp.bfloat16)
    return high, low


def rows_kernel(raw_ref, inverse_ref, out_ref, parts_ref):
    solved = dot_nt(raw_ref[...], inverse_ref[...])
    out_ref[...] = solved
    high, low = split(solved)
    parts_ref[:, :TOTAL] = high
    parts_ref[:, TOTAL : 2 * TOTAL] = high
    parts_ref[:, 2 * TOTAL :] = low


def solve_rows(raw, inverse):
    length = raw.shape[0]
    step = min(512, length)
    block = pl.BlockSpec((step, TOTAL), lambda i: (i, 0))
    return pl.pallas_call(
        rows_kernel,
        grid=(length // step,),
        out_shape=[
            jax.ShapeDtypeStruct((length, TOTAL), jnp.float32),
            jax.ShapeDtypeStruct((length, 3 * TOTAL), jnp.bfloat16),
        ],
        in_specs=[block, pl.BlockSpec((TOTAL, TOTAL), lambda i: (0, 0))],
        out_specs=[block, pl.BlockSpec((step, 3 * TOTAL), lambda i: (i, 0))],
        compiler_params=pltpu.CompilerParams(vmem_limit_bytes=24 * MIB),
    )(raw, inverse)


def cols_kernel(raw_ref, inverse_ref, out_ref, parts_ref):
    solved = dot_nt(inverse_ref[...], raw_ref[...])
    out_ref[...] = solved
    high, low = split(solved)
    parts_ref[:TOTAL] = high
    parts_ref[TOTAL : 2 * TOTAL] = low
    parts_ref[2 * TOTAL :] = high


def solve_cols(raw, inverse):
    length = raw.shape[0]
    step = min(512, length)
    block = pl.BlockSpec((TOTAL, step), lambda i: (0, i))
    return pl.pallas_call(
        cols_kernel,
        grid=(length // step,),
        out_shape=[
            jax.ShapeDtypeStruct((TOTAL, length), jnp.float32),
            jax.ShapeDtypeStruct((3 * TOTAL, length), jnp.bfloat16),
        ],
        in_specs=[
            pl.BlockSpec((step, TOTAL), lambda i: (i, 0)),
            pl.BlockSpec((TOTAL, TOTAL), lambda i: (0, 0)),
        ],
        out_specs=[block, pl.BlockSpec((3 * TOTAL, step), lambda i: (0, i))],
        compiler_params=pltpu.CompilerParams(vmem_limit_bytes=24 * MIB),
    )(raw, inverse)


def final_kernel(
    cols_blocks, runs, code_ref, run_ref, place_ref, front_ref, rows_ref, rows_parts, cols_ref, cols_parts,
    lower_ref, arrived_ref, out_ref, cursor
):
    step = pl.program_id(0)
    sources, capacity = code_ref.shape
    height, width = front_ref.shape
    unit, side = arrived_ref.shape[2:]
    per_step = height // unit

    @pl.when(step == 0)
    def _():
        for s in range(sources):
            cursor[s] = 0

    chunk = min(512, width)
    for start in range(0, width, chunk):
        at = slice(start, start + chunk)
        change = jnp.dot(rows_parts[...], cols_parts[:, at], preferred_element_type=jnp.float32)
        out_ref[:, at] = front_ref[:, at] - change

    edge = (step + 1) * per_step * cols_blocks

    @pl.loop(0, sources)
    def _(s):
        def more(k):
            code = code_ref[s, jnp.minimum(k, capacity - 1)]
            return (k < capacity) & (code >= 0) & (code < edge)

        def add(k):
            code = code_ref[s, k]
            length = run_ref[s, k]
            unit_row = code // cols_blocks - step * per_step
            columns = pl.ds(pl.multiple_of(code % cols_blocks * side, side), side)
            for run in runs:
                skipped = length // (2 * run) * (2 * run)

                @pl.when(length // run % 2 == 1)
                def _():
                    rows = pl.ds(pl.multiple_of((unit_row + skipped) * unit, unit), run * unit)
                    block = arrived_ref[s, pl.ds(k + skipped, run)]
                    out_ref[rows, columns] += block.reshape(run * unit, side)

            return k + length

        cursor[s] = lax.while_loop(more, add, cursor[s])

    top = (place_ref[0] == 0) & (step == 0)

    @pl.when(top)
    def _():
        out_ref[...] = cols_ref[...]

    @pl.when(place_ref[1] == 0)
    def _():
        out_ref[:, :TOTAL] = jnp.where(top, lower_ref[...], rows_ref[...])


def finish(front, rows, cols, lower, arrived, codes, lengths, place, cols_blocks):
    row_len, col_len = front.shape
    height = TOTAL
    smem = pl.BlockSpec(memory_space=pltpu.SMEM)
    block = pl.BlockSpec((height, TOTAL), lambda i: (i, 0))
    parts = pl.BlockSpec((height, 3 * TOTAL), lambda i: (i, 0))
    wide = pl.BlockSpec((height, col_len), lambda i: (i, 0))
    whole = pl.BlockSpec((TOTAL, col_len), lambda i: (0, 0))
    whole_parts = pl.BlockSpec((3 * TOTAL, col_len), lambda i: (0, 0))
    runs = (16, 8, 4, 2, 1) if arrived.shape[2] == UNIT else (1,)
    return pl.pallas_call(
        functools.partial(final_kernel, cols_blocks, runs),
        grid=(row_len // height,),
        out_shape=jax.ShapeDtypeStruct((row_len, col_len), jnp.float32),
        in_specs=[
            smem, smem, smem, wide, block, parts, whole, whole_parts,
            pl.BlockSpec((TOTAL, TOTAL), lambda i: (0, 0)),
            pl.BlockSpec(memory_space=pltpu.VMEM),
        ],
        out_specs=wide,
        scratch_shapes=[pltpu.SMEM((codes.shape[0],), jnp.int32)],
        compiler_params=pltpu.CompilerParams(vmem_limit_bytes=56 * MIB),
    )(codes, lengths, place, front, *rows, *cols, lower, arrived)


def factor(diagonal):
    def lower_of(block):
        return jnp.linalg.cholesky(jnp.tril(block) + jnp.tril(block, -1).T)

    def inverse_of(block):
        return jax.scipy.linalg.solve_triangular(block, jnp.eye(NB, dtype=jnp.float32), lower=True)

    first = lower_of(diagonal[:NB, :NB])
    first_inverse = inverse_of(first)
    below = dot_nt(diagonal[NB:, :NB], first_inverse)
    second = lower_of(diagonal[NB:, NB:] - dot_nt(below, below))
    second_inverse = inverse_of(second)
    corner = -jnp.dot(second_inverse, jnp.dot(below, first_inverse, precision=precise), precision=precise)
    zero = jnp.zeros((NB, NB), jnp.float32)
    return jnp.block([[first, zero], [below, second]]), jnp.block([[first_inverse, zero], [corner, second_inverse]])


def body(front, tiles, tile_block, valid_rows):
    row_len, col_len = front.shape
    row_count = lax.axis_size("row")
    col_count = lax.axis_size("col")
    device_count = row_count * col_count
    per_device = tiles.shape[0]
    side = tiles.shape[1]
    capacity = 2 * per_device // device_count
    rows_blocks = row_len // side
    cols_blocks = col_len // side
    row_now = lax.axis_index("row")
    col_now = lax.axis_index("col")
    device_now = row_now * col_count + col_now

    block_row = tile_block[0].reshape(device_count, per_device)
    block_col = tile_block[1].reshape(device_count, per_device)
    target_row = block_row // rows_blocks
    target = target_row * col_count + block_col // cols_blocks
    code = block_row % rows_blocks * cols_blocks + block_col % cols_blocks
    position = lax.broadcasted_iota(jnp.int32, target.shape, 1)
    place = jnp.stack([row_now, col_now]).astype(jnp.int32)

    def own(values):
        return lax.dynamic_index_in_dim(values, device_now, 0, keepdims=False)

    in_panel = block_col < PANELS
    panel_key = jnp.where(in_panel, target_row, -1)
    panel_rank = jnp.sum(
        (panel_key[:, :, None] == panel_key[:, None, :]) & (position[:, None, :] < position[:, :, None]),
        axis=2,
    )
    same_col = lax.dynamic_index_in_dim(
        jnp.stack([panel_key, panel_rank, code]).reshape(3, row_count, col_count, per_device),
        col_now, 2, keepdims=False,
    )

    def send_panel(tiles, valid_rows, depth):
        ahead = (own(target_row) - row_now) % row_count
        fits = own(in_panel) & (own(panel_rank) < depth)
        panel_slot = jnp.where(fits, ahead * depth + own(panel_rank), -1)
        panel_out = pack(tiles, panel_slot, valid_rows, row_count * depth)
        panel_in = [panel_out[:depth]]
        for shift in range(1, row_count):
            sending = panel_out[shift * depth : (shift + 1) * depth]
            turn = [(r, (r + shift) % row_count) for r in range(row_count)]
            panel_in.append(lax.ppermute(sending, "row", turn))
        return panel_in

    def sum_panel(front, panel_in, depth):
        fits = (same_col[0] == row_now)[:, :, None] & (same_col[1][:, :, None] == jnp.arange(depth))
        panel_code = same_col[2] // cols_blocks * PANELS + same_col[2] % cols_blocks
        panel_codes = jnp.sum(jnp.where(fits, panel_code[:, :, None] + 1, 0), axis=1) - 1
        by_shift = (row_now - jnp.arange(row_count)) % row_count
        panel_codes = jnp.take(panel_codes, by_shift, axis=0).reshape(-1)
        first = (col_now == 0).astype(jnp.int32).reshape(1)
        return raw_panel(front, jnp.concatenate(panel_in, 0), panel_codes, first)

    panel_depth = (capacity * 5 + 7) // 8
    panel_in = send_panel(tiles, valid_rows, panel_depth)

    units = side // UNIT
    length = capacity * units
    width = length * 41 // 64
    pass_on = length * 13 // 32
    half_count = device_count // 2
    half_base = device_now // half_count * half_count
    unit_rows = rows_blocks * units
    local_codes = unit_rows * cols_blocks
    own_target, own_code = own(target), own(code)
    own_position = own(position)
    filled = (valid_rows + UNIT - 1) // UNIT
    key = (own_target * rows_blocks * cols_blocks + own_code) * per_device + own_position
    before = key[None, :] < key[:, None]
    together = own_target[None, :] == own_target[:, None]
    base = jnp.sum(jnp.where(before & together, filled[None, :], 0), axis=1)
    order = jnp.sum(before, axis=1)
    unit_code = (own_target * unit_rows + own_code // cols_blocks * units) * cols_blocks
    unit_code += own_code % cols_blocks
    meta = jnp.stack([own_position, own_target, base, filled, unit_code, valid_rows])
    meta = jnp.sum(
        jnp.where(order[None, :, None] == jnp.arange(per_device), meta[:, :, None], 0), axis=1
    )
    to_device = own_target[:, None] == jnp.arange(device_count)
    load = jnp.sum(jnp.where(to_device, filled[:, None], 0), axis=0).reshape(2, half_count)
    empty = load == 0
    empty_rank = jnp.cumsum(empty, axis=1) - 1
    device_ids = jnp.arange(device_count).reshape(2, half_count)
    listed = (empty[:, :, None]) & (empty_rank[:, :, None] == jnp.arange(half_count))
    empties = jnp.sum(jnp.where(listed, device_ids[:, :, None], 0), axis=1)
    free = jnp.sum(empty, axis=1)
    left = jnp.sum(jnp.maximum(load - width, 0), axis=1)
    failed = jnp.any(left > free * width) | jnp.any(own(in_panel) & (own(panel_rank) >= panel_depth))
    counts = jnp.concatenate([jnp.sum(own_target < half_count)[None], free]).astype(jnp.int32)
    outgoing, sent_codes = spread(
        tiles, meta.astype(jnp.int32), empties.astype(jnp.int32), counts,
        device_count, width, length, cols_blocks,
    )

    partial = sum_panel(front, panel_in, panel_depth)
    partial, sent_codes = lax.optimization_barrier((partial, sent_codes))
    raw_rows = lax.psum(partial, "col")
    got = lax.all_to_all(sent_codes[:, :width], ("row", "col"), 0, 0, tiled=True)
    outgoing, got = lax.optimization_barrier((outgoing, got))
    arrived = lax.all_to_all(outgoing, ("row", "col"), 0, 0, tiled=True)
    got_target = got // local_codes
    local = got % local_codes
    mine = (got >= 0) & (got_target == device_now)
    direct_codes = jnp.where(mine, local, -1)
    steps = jnp.arange(width)
    opening = (local // cols_blocks % units == 0) | jnp.logical_not(mine)
    later = (steps[None, :] > steps[:, None]) & opening[:, None, :]
    direct_runs = jnp.min(jnp.where(later, steps, width), axis=2) - steps
    total_units = device_count * width
    passing = ((got >= 0) & (got_target != device_now)).reshape(-1)
    flat_key = jnp.where(passing, got.reshape(-1) * total_units + jnp.arange(total_units), -1)
    flat_target = jnp.where(passing, got_target.reshape(-1), -1)
    rank = jnp.sum(
        (flat_target[None, :] == flat_target[:, None]) & (flat_key[None, :] < flat_key[:, None]), axis=1
    )
    failed = failed | jnp.any(passing & (rank >= pass_on))
    relay_slot = jnp.where(
        passing & (rank < pass_on), (flat_target - half_base) * pass_on + rank, -1
    )
    picked = relay_slot[:, None] == jnp.arange(half_count * pass_on)
    relay_codes = jnp.sum(jnp.where(picked, local.reshape(-1)[:, None] + 1, 0), axis=0) - 1
    notes = jnp.zeros((2, half_count, pass_on + 1), jnp.int32)
    notes = lax.dynamic_update_slice(
        notes, relay_codes.reshape(1, half_count, pass_on).astype(jnp.int32), (device_now // half_count, 0, 0)
    )
    notes = notes.at[:, :, pass_on].set(failed.astype(jnp.int32))
    notes, arrived = lax.optimization_barrier((notes, arrived))
    notes = lax.all_to_all(
        notes.reshape(device_count, pass_on + 1), ("row", "col"), 0, 0, tiled=True
    )
    too_full = jnp.any(notes[:, pass_on] != 0)
    relay_codes = lax.dynamic_slice_in_dim(notes, half_base, half_count, 0)[:, :pass_on]
    relay_slot = relay_slot.reshape(device_count, width)

    flat = relay_codes.reshape(-1)
    unit_row, relay_col = flat // cols_blocks, flat % cols_blocks
    wanted = (flat >= 0) & ((row_now > 0) | (unit_row >= TOTAL // UNIT))
    wanted &= (col_now > 0) | (relay_col >= PANELS)
    relay_block = unit_row // units * cols_blocks + relay_col
    relay_key = jnp.where(wanted, relay_block * units + unit_row % units, local_codes)
    relay_key = relay_key * flat.shape[0] + jnp.arange(flat.shape[0])
    relay_order = jnp.sum(relay_key[None, :] < relay_key[:, None], axis=1)
    listing = jnp.stack([relay_block, unit_row % units, jnp.arange(flat.shape[0])])
    at_order = relay_order[None, :, None] == jnp.arange(flat.shape[0])
    listing = jnp.sum(jnp.where(at_order, listing[:, :, None], 0), axis=1).astype(jnp.int32)
    listing = [*listing, jnp.sum(wanted).astype(jnp.int32).reshape(1)]

    passed = relay(relay_slot, arrived, half_count * pass_on)
    slice_start = col_now * col_len % row_len
    slice_root = col_now * col_len // row_len

    def chain(raw_rows, *others):
        picked = lax.dynamic_slice_in_dim(raw_rows, slice_start, col_len, 0)
        raw_cols = lax.psum(jnp.where(row_now == slice_root, picked, 0.0), "row")
        diagonal = jnp.where(row_now == 0, raw_rows[:TOTAL], jnp.eye(TOTAL, dtype=jnp.float32))
        lower, inverse = factor(diagonal)
        known = jnp.where(row_now == 0, inverse, 0.0)
        inverse = known
        for other in range(1, row_count):
            inverse += lax.ppermute(known, "row", [(0, other)])
        rows = solve_rows(raw_rows, inverse)
        raw_cols, rows, others = lax.optimization_barrier((raw_cols, rows, others))
        return rows, solve_cols(raw_cols, inverse), lower, *others

    tables = (direct_codes, direct_runs, listing)
    rows, cols, lower, arrived, passed, tables = chain(raw_rows, arrived, passed, tables)
    direct_codes, direct_runs, listing = tables

    def relayed(front, tiles, valid_rows, arrived, passed, rows, cols, lower):
        halves = [list(range(half_count)), list(range(half_count, device_count))]
        passed = lax.all_to_all(
            passed.reshape(half_count, pass_on, UNIT, side), ("row", "col"), 0, 0,
            axis_index_groups=halves, tiled=True,
        )
        partial = finish(
            front, rows, cols, lower, arrived, direct_codes, direct_runs, place, cols_blocks
        )
        return add_relayed(partial, passed.reshape(-1, UNIT, side), listing, cols_blocks)

    def padded(front, tiles, valid_rows, arrived, passed, rows, cols, lower):
        partial = sum_panel(front, send_panel(tiles, valid_rows, capacity), capacity)
        raw_rows = lax.psum(partial, "col")
        order = (target * rows_blocks * cols_blocks + code) * per_device + position
        ranking = jnp.sum(
            (target[:, :, None] == target[:, None, :]) & (order[:, None, :] < order[:, :, None]), axis=2
        )
        slot = own(target) * capacity + own(ranking)
        here = (target == device_now)[:, :, None] & (ranking[:, :, None] == jnp.arange(capacity))
        codes = jnp.sum(jnp.where(here, code[:, :, None] + 1, 0), axis=1) - 1
        packed = pack(tiles, slot, valid_rows, device_count * capacity)
        arrived = lax.all_to_all(
            packed.reshape(device_count, capacity, side, side), ("row", "col"), 0, 0, tiled=True
        )
        rows, cols, lower = chain(raw_rows)
        return finish(
            front, rows, cols, lower, arrived, codes, jnp.ones_like(codes), place, cols_blocks
        )

    return lax.cond(
        too_full, padded, relayed, front, tiles, valid_rows, arrived, passed, rows, cols, lower
    )


def solution(mesh):
    placed = (P("row", "col"), P(("row", "col"), None, None), P(), P(("row", "col")))
    return jax.shard_map(
        body, mesh=mesh, in_specs=placed, out_specs=P("row", "col"), check_vma=False
    )
```

profile of v0, /device:TPU:7, one launch (start us, length us, event | category | flops | bytes accessed | tf_op | source)
XLA Modules:
  0.0 500.1 jit_solution(5828629170490015939)
XLA Ops:
  9.4 7.1 %shard_map.49 = f32[20,128,128]{2,1,0:T(8,128)S(1)} custom-call(s32[128]{0:T(128)S(1)} %get-tuple-element.284.slot_ref, s32[128]{0:T(128)} %valid_ref.1, f32[128,128,128]{2,1,0:T(8,128)} %tiles_ref.1), custom_call_target="tpu_custom_call" | custom-call | tf_op jit(solution)/shard_map/pallas_call | solution.py:56
  16.6 3.7 collective-permute-start.8
  24.0 21.1 %shard_map.48 = (f32[32,82,8,128]{3,2,1,0:T(8,128)S(1)}, s32[32,128]{1,0:T(8,128)S(1)}) custom-call(s32[6,128]{1,0:T(8,128)S(1)} %select_reduce_fusion.7.meta_ref, s32[2,16]{1,0:T(2,128)S(1)} %select_reduce_fusion.11.empty_ref, s32[3]{0:T(128)S(1)} %pad_add_fusion.1.count_ref, f32[128,16,8,128]{3,2,1,0:T(8,128)} %bitcast.151), custom_call_target="tpu_custom_call" | custom-call | tf_op jit(solution)/shard_map/pallas_call | solution.py:122
  45.0 4.2 copy-done.3
  49.3 3.0 shard_map.50
  52.3 1.9 copy-done.1
  54.2 9.9 %all_to_all.37 = s32[32,1,82]{2,1,0:T(1,128)S(1)} all-to-all(s32[32,1,82]{2,1,0:T(1,128)S(1)} %bitcast.150), channel_id=1, replica_groups=mesh['row'=4,'col'=8] {'row','col'}, dimensions={0} | all-to-all | bytes 20992 | tf_op jit(solution)/shard_map/all_to_all | solution.py:552
  64.1 6.0 %all-to-all-start.3 = ((f32[32,82,8,128]{3,2,1,0:T(8,128)}), f32[32,82,8,128]{3,2,1,0:T(8,128)}, u32[]{:S(2)}, u32[]{:S(2)}) async-start(f32[32,82,8,128]{3,2,1,0:T(8,128)} %copy-done.3), calls=%async_computation.3 | async-start | bytes 21495808 | tf_op jit(solution)/shard_map/all_to_all | solution.py:554
  74.7 6.1 %convert_reduce_fusion.1 = s32[2624]{0:T(1024)S(1)} fusion(s32[2624]{0:T(1024)S(1)} %get-tuple-element.283, s32[2624]{0:T(1024)S(1)} %get-tuple-element.282), kind=kLoop, calls=%fused_computation.99 | loop fusion | flops 34424256 | bytes 31488 | tf_op jit(solution)/shard_map/reduce_sum | solution.py:567
  85.2 1.6 scatter.4
  86.8 1.5 select_reduce_fusion.6
  88.3 170.8 %all-reduce.13.cloned.1.call-done.raw_ref = f32[4096,256]{1,0:T(8,128)} async-done(((f32[4096,256]{1,0:T(8,128)}), f32[4096,256]{1,0:T(8,128)}) %all-reduce.13.cloned.1.call-update) | async-done | bytes 4194320 | tf_op jit(solution)/shard_map/psum | solution.py:551
  260.5 11.7 %cholesky.96 = f32[128,128]{1,0:T(8,128)S(1)} custom-call(f32[128,128]{1,0:T(8,128)S(1)} %copy.125), custom_call_target="Cholesky" | custom-call | tf_op jit(solution)/shard_map/jit(cholesky)/cholesky | solution.py:436
  273.6 9.8 %custom-call.10 = f32[1,128,128]{1,2,0:T(8,128)S(1)} custom-call(f32[1,128,128]{2,1,0:T(8,128)S(1)} %get-tuple-element.250), custom_call_target="InvertDiagBlocksLowerTriangular" | custom-call | tf_op jit(solution)/shard_map/jit(_solve_triangular)/triangular_solve | solution.py:439
  284.6 11.9 %cholesky.107 = f32[128,128]{1,0:T(8,128)S(1)} custom-call(f32[128,128]{1,0:T(8,128)S(1)} %fusion.44), custom_call_target="Cholesky" | custom-call | tf_op jit(solution)/shard_map/jit(cholesky)/cholesky | solution.py:436
  297.9 9.8 %custom-call.11 = f32[1,128,128]{1,2,0:T(8,128)S(1)} custom-call(f32[1,128,128]{2,1,0:T(8,128)S(1)} %get-tuple-element.248), custom_call_target="InvertDiagBlocksLowerTriangular" | custom-call | tf_op jit(solution)/shard_map/jit(_solve_triangular)/triangular_solve | solution.py:439
  308.7 15.4 %collective-permute-start.10 = (f32[256,256]{1,0:T(8,128)S(1)}, f32[256,256]{1,0:T(8,128)S(1)}, u32[]{:S(2)}, u32[]{:S(2)}) collective-permute-start(f32[256,256]{1,0:T(8,128)S(1)} %fusion.35), channel_id=1, source_target_pairs={{0,16},{1,17},{2,18},{3,19},{4,20},{5,21},{6,22},{7,23}} | collective-permute-start | bytes 786440 | tf_op jit(solution)/shard_map/ppermute | solution.py:614
  326.6 3.0 dynamic-slice_select_fusion.1
  330.4 3.2 all-to-all-start.4
  333.7 2.7 collective-permute-done.11
  336.4 11.2 %collective-permute-done.9 = f32[256,256]{1,0:T(8,128)S(1)} collective-permute-done((f32[256,256]{1,0:T(8,128)S(1)}, f32[256,256]{1,0:T(8,128)S(1)}, u32[]{:S(2)}, u32[]{:S(2)}) %collective-permute-start.9) | collective-permute-done | bytes 262176 | tf_op jit(solution)/shard_map/ppermute | solution.py:614
  347.7 2.2 copy-done.4
  349.9 7.5 %shard_map.51 = (f32[4096,256]{1,0:T(8,128)}, bf16[4096,768]{1,0:T(8,128)(2,1)}) custom-call(f32[4096,256]{1,0:T(8,128)S(1)} %copy-done.4, f32[256,256]{1,0:T(8,128)S(1)} %add_add_fusion.1.inverse_ref), custom_call_target="tpu_custom_call" | custom-call | tf_op jit(solution)/shard_map/pallas_call | solution.py:309
  357.4 11.0 %shard_map.52 = f32[832,8,128]{2,1,0:T(8,128)} custom-call(s32[32,82]{1,0:T(8,128)S(1)} %add_select_fusion.13.slot_ref, f32[32,82,8,128]{3,2,1,0:T(8,128)} %all-to-all-done.3.arrived_ref), custom_call_target="tpu_custom_call" | custom-call | tf_op jit(solution)/shard_map/pallas_call | solution.py:155
  372.8 47.8 %all-reduce.15.cloned.1.call-done.raw_ref = f32[2048,256]{1,0:T(8,128)} async-done(((f32[2048,256]{1,0:T(8,128)}), f32[2048,256]{1,0:T(8,128)}) %all-reduce.15.cloned.1.call-update) | async-done | bytes 2097168 | tf_op jit(solution)/shard_map/psum | solution.py:608
  420.7 1.6 copy-done.9
  422.2 4.2 shard_map.53
  426.4 66.3 %conditional.1 = (f32[4096,2048]{1,0:T(8,128)}) conditional(s32[]{:T(128)} %convert_element_type.63, (s32[32,82]{1,0:T(8,128)S(1)}, s32[32,82]{0,1:T(8,128)S(1)}, s32[2]{0:T(128)}, f32[4096,2048]{1,0:T(8,128)}, f32[4096,256]{1,0:T(8,128)}, /*index=5*/bf16[4096,768]{1,0:T(8,128)(2,1)}, f32[256,2048]{1,0:T(8,128)}, bf16[768,2048]{1,0:T(8,128)(2,1)}, ...), branch_computations={%region_25.28_spmd, %region_26.34_spmd} | conditional | flops 159337888 | bytes 288581216 | solution.py:653
  426.4 4.7 all-to-all-start
  431.8 47.8 %branch_0_fun.2.partial_ref = f32[4096,2048]{1,0:T(8,128)} custom-call(s32[32,82]{1,0:T(8,128)S(1)} %get-tuple-element.89.code_ref, s32[32,82]{1,0:T(8,128)} %copy.134.run_ref, s32[2]{0:T(128)S(1)} %copy-done.16, f32[4096,2048]{1,0:T(8,128)} %get-tuple-element.92.front_ref, f32[4096,256]{1,0:T(8,128)} %get-tuple-element.93.rows_ref, ...), custom_call_target="tpu_custom_call" | custom-call | tf_op jit(solution)/shard_map/cond/branch_0_fun/pallas_call | solution.py:419
  479.6 3.1 all-to-all-done
  482.7 8.9 %branch_0_fun.3 = f32[4096,2048]{1,0:T(8,128)} custom-call(s32[832]{0:T(1024)S(1)} %get-tuple-element.85.block_ref, s32[832]{0:T(1024)S(1)} %get-tuple-element.86.unit_ref, s32[832]{0:T(1024)S(1)} %get-tuple-element.87.index_ref, s32[1]{0:T(128)} %get-tuple-element.88.count_ref, ...), custom_call_target="tpu_custom_call", output_to_operand_aliasing={{}: (4, {})} | custom-call | tf_op jit(solution)/shard_map/cond/branch_0_fun/pallas_call | solution.py:234
  (141 shorter events, 27.4 us)
Async XLA Ops:
  7.4 9.0 %copy-start.12 = (s32[32,128]{1,0:T(8,128)}, s32[32,128]{1,0:T(8,128)S(1)}, u32[]{:S(2)}) copy-start(s32[32,128]{1,0:T(8,128)S(1)} %get-tuple-element.277) | copy-start | bytes 49156
  7.5 63.9 %copy-start.15 = (pred[32,128]{1,0:T(8,128)(4,1)}, pred[32,128]{1,0:T(8,128)(4,1)S(1)}, u32[]{:S(2)}) copy-start(pred[32,128]{1,0:T(8,128)(4,1)S(1)} %get-tuple-element.253) | copy-start | bytes 12292
  9.4 11.5 %copy-start.13 = (s32[128]{0:T(128)S(1)}, s32[128]{0:T(128)}, u32[]{:S(2)}) copy-start(s32[128]{0:T(128)} %valid_ref.1) | copy-start | bytes 1540
  16.6 32.6 %collective-permute-start.8 = (f32[5,128,128]{2,1,0:T(8,128)S(1)}, f32[5,128,128]{2,1,0:T(8,128)S(1)}, u32[]{:S(2)}, u32[]{:S(2)}) collective-permute-start(f32[5,128,128]{2,1,0:T(8,128)S(1)} %get-tuple-element.263), channel_id=1, source_target_pairs={{0,24},{8,0},{16,8},{24,16},{1,25},{9,1},{17,9},{25,17},{2,26},{10... | collective-permute-start | bytes 983048 | tf_op jit(solution)/shard_map/ppermute | solution.py:496
  20.3 28.9 %collective-permute-start.7 = (f32[5,128,128]{2,1,0:T(8,128)S(1)}, f32[5,128,128]{2,1,0:T(8,128)S(1)}, u32[]{:S(2)}, u32[]{:S(2)}) collective-permute-start(f32[5,128,128]{2,1,0:T(8,128)S(1)} %get-tuple-element.264), channel_id=1, source_target_pairs={{0,16},{8,24},{16,0},{24,8},{1,17},{9,25},{17,1},{25,9},{2,18},{10... | collective-permute-start | bytes 983048 | tf_op jit(solution)/shard_map/ppermute | solution.py:496
  20.3 28.9 %collective-permute-start.6 = (f32[5,128,128]{2,1,0:T(8,128)S(1)}, f32[5,128,128]{2,1,0:T(8,128)S(1)}, u32[]{:S(2)}, u32[]{:S(2)}) collective-permute-start(f32[5,128,128]{2,1,0:T(8,128)S(1)} %get-tuple-element.265), channel_id=1, source_target_pairs={{0,8},{8,16},{16,24},{24,0},{1,9},{9,17},{17,25},{25,1},{2,10},{10... | collective-permute-start | bytes 983048 | tf_op jit(solution)/shard_map/ppermute | solution.py:496
  45.0 4.2 copy-start.3
  52.3 1.9 copy-start.1
  64.1 266.3 %all-to-all-start.3 = ((f32[32,82,8,128]{3,2,1,0:T(8,128)}), f32[32,82,8,128]{3,2,1,0:T(8,128)}, u32[]{:S(2)}, u32[]{:S(2)}) async-start(f32[32,82,8,128]{3,2,1,0:T(8,128)} %copy-done.3), calls=%async_computation.3 | async-start | bytes 21495808 | tf_op jit(solution)/shard_map/all_to_all | solution.py:554
  70.1 189.1 %all-reduce.13.cloned.1.call-start = ((), (), s32[]{:S(2)}) async-start(), calls=%async_computation.7 | async-start | bytes 8388608 | tf_op jit(solution)/shard_map/psum | solution.py:551
  74.1 346.6 %all-reduce.15.cloned.1.call-start = ((), (), s32[]{:S(2)}) async-start(), calls=%async_computation.8 | async-start | bytes 4194304 | tf_op jit(solution)/shard_map/psum | solution.py:608
  308.7 25.0 %collective-permute-start.10 = (f32[256,256]{1,0:T(8,128)S(1)}, f32[256,256]{1,0:T(8,128)S(1)}, u32[]{:S(2)}, u32[]{:S(2)}) collective-permute-start(f32[256,256]{1,0:T(8,128)S(1)} %fusion.35), channel_id=1, source_target_pairs={{0,16},{1,17},{2,18},{3,19},{4,20},{5,21},{6,22},{7,23}} | collective-permute-start | bytes 786440 | tf_op jit(solution)/shard_map/ppermute | solution.py:614
  324.0 12.4 %collective-permute-start.11 = (f32[256,256]{1,0:T(8,128)S(1)}, f32[256,256]{1,0:T(8,128)S(1)}, u32[]{:S(2)}, u32[]{:S(2)}) collective-permute-start(f32[256,256]{1,0:T(8,128)S(1)} %fusion.35), channel_id=1, source_target_pairs={{0,24},{1,25},{2,26},{3,27},{4,28},{5,29},{6,30},{7,31}} | collective-permute-start | bytes 786440 | tf_op jit(solution)/shard_map/ppermute | solution.py:614
  325.3 22.3 %collective-permute-start.9 = (f32[256,256]{1,0:T(8,128)S(1)}, f32[256,256]{1,0:T(8,128)S(1)}, u32[]{:S(2)}, u32[]{:S(2)}) collective-permute-start(f32[256,256]{1,0:T(8,128)S(1)} %fusion.35), channel_id=1, source_target_pairs={{0,8},{1,9},{2,10},{3,11},{4,12},{5,13},{6,14},{7,15}} | collective-permute-start | bytes 786440 | tf_op jit(solution)/shard_map/ppermute | solution.py:614
  330.4 37.9 %all-to-all-start.4 = ((s32[32,1,53]{2,1,0:T(1,128)}), s32[32,1,53]{2,1,0:T(1,128)S(1)}, u32[]{:S(2)}, u32[]{:S(2)}) async-start(s32[32,1,53]{2,1,0:T(1,128)} %bitcast.45), calls=%async_computation.4 | async-start | bytes 32768 | tf_op jit(solution)/shard_map/all_to_all | solution.py:582
  347.7 2.2 copy-start.4
  420.6 1.6 copy-start.9
  426.4 5.3 %copy-start.16 = (s32[2]{0:T(128)S(1)}, s32[2]{0:T(128)}, u32[]{:S(2)}) copy-start(s32[2]{0:T(128)} %get-tuple-element.91.place_ref) | copy-start | bytes 28 | tf_op jit(solution)/shard_map/cond
  426.4 56.3 %all-to-all-start = ((f32[16,52,8,128]{3,2,1,0:T(8,128)}), f32[16,52,8,128]{3,2,1,0:T(8,128)S(1)}, u32[]{:S(2)}, u32[]{:S(2)}) async-start(f32[16,52,8,128]{3,2,1,0:T(8,128)} %bitcast.152), calls=%async_computation | async-start | bytes 6815744 | tf_op jit(solution)/shard_map/cond/branch_0_fun/all_to_all | solution.py:625
Sparse Core Ops, SparseCore 0:
  74.2 184.9 all-reduce.12
  329.8 90.7 all-reduce.14
where the time goes:
time: 509 us; the launch traced here: 500 us
  waiting for transfers between devices  236 us (46%)
  Pallas kernels  111 us (22%)
  other arithmetic  70 us (14%)
  starting transfers between devices  36.2 us (7%)
  local copies, waits for them, and re-layouts  17.6 us (3%)
  between operations  17.3 us (3%)
  blocking collectives  9.87 us (2%)
    psum x1, waiting for transfers between devices, body(): raw_rows = lax.psum(partial, 'col')  171 us
    psum x1, waiting for transfers between devices, chain(): raw_cols = lax.psum(jnp.where(row_now == slice_root, picked, 0.0), 'row')  47.8 us
    pallas_call x1, Pallas kernels, finish(): pl.pallas_call(functools.partial(final_kernel, cols_blocks, runs), grid=(...  47.8 us
    another operation x6, other arithmetic, lower_of(): return jnp.linalg.cholesky(jnp.tril(block) + jnp.tril(block, -1).T)  25.1 us
    pallas_call x1, Pallas kernels, spread(): pl.pallas_call(functools.partial(spread_kernel, width, stride), out_shape...  21.1 us
    another operation x5, other arithmetic, inverse_of(): jax.scipy.linalg.solve_triangular(block, jnp.eye(NB, dtype=jnp.float32),...  20.9 us
    ppermute x3, starting transfers between devices, chain(): inverse += lax.ppermute(known, 'row', [(0, other)])  18 us
    ppermute x3, waiting for transfers between devices, chain(): inverse += lax.ppermute(known, 'row', [(0, other)])  14 us
  transfers between devices with their start and end apart: 11, of which 5 were waited for; matrix products, arithmetic and copies ran while one was open for 15% of the time, Pallas kernels for 17%

commit v1 on v0

--- a/solution.py
+++ b/solution.py
@@ -319,8 +319,8 @@
     )(raw, inverse)
 
 
-def cols_kernel(raw_ref, inverse_ref, out_ref, parts_ref):
-    solved = dot_nt(inverse_ref[...], raw_ref[...])
+def cols_kernel(order_ref, raw_ref, inverse_ref, out_ref, parts_ref):
+    solved = dot_nt(inverse_ref[...], raw_ref[0])
     out_ref[...] = solved
     high, low = split(solved)
     parts_ref[:TOTAL] = high
@@ -328,24 +328,30 @@
     parts_ref[2 * TOTAL :] = high
 
 
-def solve_cols(raw, inverse):
-    length = raw.shape[0]
-    step = min(512, length)
-    block = pl.BlockSpec((TOTAL, step), lambda i: (0, i))
+def solve_cols(chunks, order, inverse):
+    count, step = chunks.shape[:2]
+    length = count * step
+    grid_spec = pltpu.PrefetchScalarGridSpec(
+        num_scalar_prefetch=1,
+        grid=(count,),
+        in_specs=[
+            pl.BlockSpec((1, step, TOTAL), lambda i, order: (order[i], 0, 0)),
+            pl.BlockSpec((TOTAL, TOTAL), lambda i, order: (0, 0)),
+        ],
+        out_specs=[
+            pl.BlockSpec((TOTAL, step), lambda i, order: (0, i)),
+            pl.BlockSpec((3 * TOTAL, step), lambda i, order: (0, i)),
+        ],
+    )
     return pl.pallas_call(
         cols_kernel,
-        grid=(length // step,),
+        grid_spec=grid_spec,
         out_shape=[
             jax.ShapeDtypeStruct((TOTAL, length), jnp.float32),
             jax.ShapeDtypeStruct((3 * TOTAL, length), jnp.bfloat16),
         ],
-        in_specs=[
-            pl.BlockSpec((step, TOTAL), lambda i: (i, 0)),
-            pl.BlockSpec((TOTAL, TOTAL), lambda i: (0, 0)),
-        ],
-        out_specs=[block, pl.BlockSpec((3 * TOTAL, step), lambda i: (0, i))],
         compiler_params=pltpu.CompilerParams(vmem_limit_bytes=24 * MIB),
-    )(raw, inverse)
+    )(order, chunks, inverse)
 
 
 def final_kernel(
@@ -504,6 +510,11 @@
         panel_codes = jnp.take(panel_codes, by_shift, axis=0).reshape(-1)
         first = (col_now == 0).astype(jnp.int32).reshape(1)
         return raw_panel(front, jnp.concatenate(panel_in, 0), panel_codes, first)
+
+    def gather_panel(partial):
+        chunk = lax.psum_scatter(partial, "col", scatter_dimension=0, tiled=True)
+        gathered = lax.all_gather(chunk, "row", axis=0)
+        return gathered, lax.all_gather(chunk, "col", axis=0, tiled=True)
 
     panel_depth = (capacity * 5 + 7) // 8
     panel_in = send_panel(tiles, valid_rows, panel_depth)
@@ -548,7 +559,7 @@
 
     partial = sum_panel(front, panel_in, panel_depth)
     partial, sent_codes = lax.optimization_barrier((partial, sent_codes))
-    raw_rows = lax.psum(partial, "col")
+    gathered, raw_rows = gather_panel(partial)
     got = lax.all_to_all(sent_codes[:, :width], ("row", "col"), 0, 0, tiled=True)
     outgoing, got = lax.optimization_barrier((outgoing, got))
     arrived = lax.all_to_all(outgoing, ("row", "col"), 0, 0, tiled=True)
@@ -600,24 +611,33 @@
     listing = [*listing, jnp.sum(wanted).astype(jnp.int32).reshape(1)]
 
     passed = relay(relay_slot, arrived, half_count * pass_on)
-    slice_start = col_now * col_len % row_len
-    slice_root = col_now * col_len // row_len
-
-    def chain(raw_rows, *others):
-        picked = lax.dynamic_slice_in_dim(raw_rows, slice_start, col_len, 0)
-        raw_cols = lax.psum(jnp.where(row_now == slice_root, picked, 0.0), "row")
+    def chain(gathered, raw_rows, arrived):
+        gathered, raw_rows = lax.optimization_barrier((gathered, raw_rows))
         diagonal = jnp.where(row_now == 0, raw_rows[:TOTAL], jnp.eye(TOTAL, dtype=jnp.float32))
         lower, inverse = factor(diagonal)
         known = jnp.where(row_now == 0, inverse, 0.0)
+        gathered, arrived = lax.optimization_barrier((gathered, arrived))
+        share = col_count // row_count
+        chunks = []
+        for turn in range(row_count):
+            pairs = [
+                (h * row_count + i, (i + turn) % row_count * share + h)
+                for h in range(share)
+                for i in range(row_count)
+            ]
+            sending = lax.dynamic_index_in_dim(gathered, (col_now + turn) % row_count, 0, keepdims=False)
+            chunks.append(lax.ppermute(sending, "col", pairs))
+        order = (col_now // share - jnp.arange(row_count)) % row_count
         inverse = known
         for other in range(1, row_count):
             inverse += lax.ppermute(known, "row", [(0, other)])
         rows = solve_rows(raw_rows, inverse)
-        raw_cols, rows, others = lax.optimization_barrier((raw_cols, rows, others))
-        return rows, solve_cols(raw_cols, inverse), lower, *others
+        cols = solve_cols(jnp.stack(chunks), order.astype(jnp.int32), inverse)
+        return rows, cols, lower
 
     tables = (direct_codes, direct_runs, listing)
-    rows, cols, lower, arrived, passed, tables = chain(raw_rows, arrived, passed, tables)
+    rows, cols, lower = chain(gathered, raw_rows, arrived)
+    rows, cols, lower, passed, tables = lax.optimization_barrier((rows, cols, lower, passed, tables))
     direct_codes, direct_runs, listing = tables
 
     def relayed(front, tiles, valid_rows, arrived, passed, rows, cols, lower):
@@ -633,7 +653,7 @@
 
     def padded(front, tiles, valid_rows, arrived, passed, rows, cols, lower):
         partial = sum_panel(front, send_panel(tiles, valid_rows, capacity), capacity)
-        raw_rows = lax.psum(partial, "col")
+        gathered, raw_rows = gather_panel(partial)
         order = (target * rows_blocks * cols_blocks + code) * per_device + position
         ranking = jnp.sum(
             (target[:, :, None] == target[:, None, :]) & (order[:, None, :] < order[:, :, None]), axis=2
@@ -645,7 +665,7 @@
         arrived = lax.all_to_all(
             packed.reshape(device_count, capacity, side, side), ("row", "col"), 0, 0, tiled=True
         )
-        rows, cols, lower = chain(raw_rows)
+        rows, cols, lower = chain(gathered, raw_rows, arrived)
         return finish(
             front, rows, cols, lower, arrived, codes, jnp.ones_like(codes), place, cols_blocks
         )

time: 509 us -> 545 us (1.071)
  waiting for transfers between devices: 236 us -> 268 us
    psum x2 -> x0, waiting for transfers between devices: 219 us -> none  [the longest x1 171 us: body(): raw_rows = lax.psum(partial, 'col')]
    all_gather x0 -> x2, waiting for transfers between devices: none -> 138 us  [the longest x1 80.6 us: gather_panel(): gathered = lax.all_gather(chunk, 'row', axis=0)]
    reduce_scatter x0 -> x1, waiting for transfers between devices: none -> 115 us  [gather_panel(): chunk = lax.psum_scatter(partial, 'col', scatter_dimension=0, tiled=True)]
    ppermute x3, starting transfers between devices: 18 us -> 6.19 us  [chain(): inverse += lax.ppermute(known, 'row', [(0, other)])]
    ppermute x0 -> x4, starting transfers between devices: none -> 10.1 us  [chain(): chunks.append(lax.ppermute(sending, 'col', pairs))]
  transfers between devices with their start and end apart: 11 -> 16, of which waited for: 5 -> 7; matrix products, arithmetic and copies ran while one was open for 15% -> 14% of each run, Pallas kernels for 17% -> 16%
where the time goes in v1:
time: 545 us; the launch traced here: 537 us
  waiting for transfers between devices  268 us (49%)
  Pallas kernels  113 us (21%)
  other arithmetic  67.3 us (12%)
  starting transfers between devices  40.4 us (7%)
  local copies, waits for them, and re-layouts  18.4 us (3%)
  between operations  16.8 us (3%)
  blocking collectives  10.7 us (2%)
    reduce_scatter x1, waiting for transfers between devices, gather_panel(): chunk = lax.psum_scatter(partial, 'col', scatter_dimension=0, tiled=True)  115 us
    all_gather x1, waiting for transfers between devices, gather_panel(): gathered = lax.all_gather(chunk, 'row', axis=0)  80.6 us
    all_gather x1, waiting for transfers between devices, gather_panel(): return (gathered, lax.all_gather(chunk, 'col', axis=0, tiled=True))  57.4 us
    pallas_call x1, Pallas kernels, finish(): pl.pallas_call(functools.partial(final_kernel, cols_blocks, runs), grid=(...  48.6 us
    another operation x6, other arithmetic, lower_of(): return jnp.linalg.cholesky(jnp.tril(block) + jnp.tril(block, -1).T)  25.2 us
    pallas_call x1, Pallas kernels, spread(): pl.pallas_call(functools.partial(spread_kernel, width, stride), out_shape...  20.9 us
    another operation x5, other arithmetic, inverse_of(): jax.scipy.linalg.solve_triangular(block, jnp.eye(NB, dtype=jnp.float32),...  20.9 us
    ppermute x3, waiting for transfers between devices, chain(): inverse += lax.ppermute(known, 'row', [(0, other)])  11.2 us
  transfers between devices with their start and end apart: 16, of which 7 were waited for; matrix products, arithmetic and copies ran while one was open for 14% of the time, Pallas kernels for 16%

profile of v1, /device:TPU:7, one launch (start us, length us, event | category | flops | bytes accessed | tf_op | source)
XLA Modules:
  0.0 537.0 jit_solution(8887137984819433139)
XLA Ops:
  9.4 7.0 %shard_map.49 = f32[20,128,128]{2,1,0:T(8,128)S(1)} custom-call(s32[128]{0:T(128)S(1)} %get-tuple-element.288.slot_ref, s32[128]{0:T(128)} %valid_ref.1, f32[128,128,128]{2,1,0:T(8,128)} %tiles_ref.1), custom_call_target="tpu_custom_call" | custom-call | tf_op jit(solution)/shard_map/pallas_call | solution.py:56
  16.5 3.3 collective-permute-start.12
  23.8 20.9 %shard_map.48 = (f32[32,82,8,128]{3,2,1,0:T(8,128)S(1)}, s32[32,128]{1,0:T(8,128)S(1)}) custom-call(s32[6,128]{1,0:T(8,128)S(1)} %select_reduce_fusion.7.meta_ref, s32[2,16]{1,0:T(2,128)S(1)} %select_reduce_fusion.11.empty_ref, s32[3]{0:T(128)S(1)} %pad_add_fusion.1.count_ref, f32[128,16,8,128]{3,2,1,0:T(8,128)} %bitcast.179), custom_call_target="tpu_custom_call" | custom-call | tf_op jit(solution)/shard_map/pallas_call | solution.py:122
  44.7 4.2 copy-done.3
  49.0 3.0 shard_map.50
  52.0 1.9 copy-done.1
  54.0 10.7 %all_to_all.37 = s32[32,1,82]{2,1,0:T(1,128)S(1)} all-to-all(s32[32,1,82]{2,1,0:T(1,128)S(1)} %bitcast.178), channel_id=1, replica_groups=mesh['row'=4,'col'=8] {'row','col'}, dimensions={0} | all-to-all | bytes 20992 | tf_op jit(solution)/shard_map/all_to_all | solution.py:563
  64.6 6.0 %all-to-all-start.3 = ((f32[32,82,8,128]{3,2,1,0:T(8,128)}), f32[32,82,8,128]{3,2,1,0:T(8,128)}, u32[]{:S(2)}, u32[]{:S(2)}) async-start(f32[32,82,8,128]{3,2,1,0:T(8,128)} %copy-done.3), calls=%async_computation.4 | async-start | bytes 21495808 | tf_op jit(solution)/shard_map/all_to_all | solution.py:565
  70.7 115.2 %reduce-scatter.5.cloned.1.call-done = f32[512,256]{1,0:T(8,128)} async-done(((f32[4096,256]{1,0:T(8,128)}), f32[512,256]{1,0:T(8,128)}) %reduce-scatter.5.cloned.1.call-update) | async-done | bytes 524304 | tf_op jit(solution)/shard_map/reduce_scatter | solution.py:515
  191.6 6.0 %convert_reduce_fusion.1 = s32[2624]{0:T(1024)S(1)} fusion(s32[2624]{0:T(1024)S(1)} %get-tuple-element.287, s32[2624]{0:T(1024)S(1)} %get-tuple-element.286), kind=kLoop, calls=%fused_computation.109 | loop fusion | flops 34424256 | bytes 31488 | tf_op jit(solution)/shard_map/reduce_sum | solution.py:578
  205.3 80.6 %all-gather.13.cloned.1.call-done = f32[2048,256]{1,0:T(8,128)} async-done(((f32[512,256]{1,0:T(8,128)}), f32[2048,256]{1,0:T(8,128)}) %all-gather.13.cloned.1.call-update) | async-done | bytes 2097168 | tf_op jit(solution)/shard_map/all_gather | solution.py:516
  285.9 57.4 %all-gather.11.cloned.1.call-done.raw_ref = f32[4096,256]{1,0:T(8,128)} async-done(((f32[512,256]{1,0:T(8,128)}), f32[4096,256]{1,0:T(8,128)}) %all-gather.11.cloned.1.call-update) | async-done | bytes 4194320 | tf_op jit(solution)/shard_map/all_gather | solution.py:517
  344.7 11.7 %cholesky.96 = f32[128,128]{1,0:T(8,128)S(1)} custom-call(f32[128,128]{1,0:T(8,128)S(1)} %copy.125), custom_call_target="Cholesky" | custom-call | tf_op jit(solution)/shard_map/jit(cholesky)/cholesky | solution.py:442
  357.8 9.8 %custom-call.10 = f32[1,128,128]{1,2,0:T(8,128)S(1)} custom-call(f32[1,128,128]{2,1,0:T(8,128)S(1)} %get-tuple-element.246), custom_call_target="InvertDiagBlocksLowerTriangular" | custom-call | tf_op jit(solution)/shard_map/jit(_solve_triangular)/triangular_solve | solution.py:445
  368.7 12.0 %cholesky.107 = f32[128,128]{1,0:T(8,128)S(1)} custom-call(f32[128,128]{1,0:T(8,128)S(1)} %fusion.47), custom_call_target="Cholesky" | custom-call | tf_op jit(solution)/shard_map/jit(cholesky)/cholesky | solution.py:442
  382.1 9.8 %custom-call.11 = f32[1,128,128]{1,2,0:T(8,128)S(1)} custom-call(f32[1,128,128]{2,1,0:T(8,128)S(1)} %get-tuple-element.244), custom_call_target="InvertDiagBlocksLowerTriangular" | custom-call | tf_op jit(solution)/shard_map/jit(_solve_triangular)/triangular_solve | solution.py:445
  394.2 3.6 collective-permute-start.15
  399.9 5.6 %collective-permute-done.15 = f32[256,256]{1,0:T(8,128)S(1)} collective-permute-done((f32[256,256]{1,0:T(8,128)S(1)}, f32[256,256]{1,0:T(8,128)S(1)}, u32[]{:S(2)}, u32[]{:S(2)}) %collective-permute-start.15) | collective-permute-done | bytes 262176 | tf_op jit(solution)/shard_map/ppermute | solution.py:633
  405.6 5.6 %collective-permute-done.13 = f32[256,256]{1,0:T(8,128)S(1)} collective-permute-done((f32[256,256]{1,0:T(8,128)S(1)}, f32[256,256]{1,0:T(8,128)S(1)}, u32[]{:S(2)}, u32[]{:S(2)}) %collective-permute-start.13) | collective-permute-done | bytes 262176 | tf_op jit(solution)/shard_map/ppermute | solution.py:633
  411.2 2.2 copy-done.5
  413.4 7.5 %shard_map.51 = (f32[4096,256]{1,0:T(8,128)}, bf16[4096,768]{1,0:T(8,128)(2,1)}) custom-call(f32[4096,256]{1,0:T(8,128)S(1)} %copy-done.5, f32[256,256]{1,0:T(8,128)S(1)} %add_add_fusion.1.inverse_ref), custom_call_target="tpu_custom_call" | custom-call | tf_op jit(solution)/shard_map/pallas_call | solution.py:309
  420.9 6.6 %all-to-all-start.4 = ((s32[32,1,53]{2,1,0:T(1,128)}), s32[32,1,53]{2,1,0:T(1,128)S(1)}, u32[]{:S(2)}, u32[]{:S(2)}) async-start(s32[32,1,53]{2,1,0:T(1,128)} %bitcast.54), calls=%async_computation.5 | async-start | bytes 32768 | tf_op jit(solution)/shard_map/all_to_all | solution.py:593
  428.7 1.7 collective-permute-start.16
  430.3 3.6 collective-permute-start.19
  434.4 4.4 collective-permute-start.17
  438.8 10.2 %shard_map.53 = f32[832,8,128]{2,1,0:T(8,128)} custom-call(s32[32,82]{1,0:T(8,128)S(1)} %add_select_fusion.13.slot_ref, f32[32,82,8,128]{3,2,1,0:T(8,128)} %all-to-all-done.3.arrived_ref), custom_call_target="tpu_custom_call" | custom-call | tf_op jit(solution)/shard_map/pallas_call | solution.py:155
  454.8 4.8 shard_map.52
  459.6 70.7 %conditional.1 = (f32[4096,2048]{1,0:T(8,128)}) conditional(s32[]{:T(128)} %convert_element_type.63, (s32[32,82]{1,0:T(8,128)S(1)}, s32[32,82]{0,1:T(8,128)S(1)}, s32[2]{0:T(128)}, f32[4096,2048]{1,0:T(8,128)}, f32[4096,256]{1,0:T(8,128)}, /*index=5*/bf16[4096,768]{1,0:T(8,128)(2,1)}, f32[256,2048]{1,0:T(8,128)}, bf16[768,2048]{1,0:T(8,128)(2,1)}, ...), branch_computations={%region_24.27_spmd, %region_25.32_spmd} | conditional | flops 158813648 | bytes 299854496 | solution.py:673
  459.6 7.3 %all-to-all-start = ((f32[16,52,8,128]{3,2,1,0:T(8,128)}), f32[16,52,8,128]{3,2,1,0:T(8,128)S(1)}, u32[]{:S(2)}, u32[]{:S(2)}) async-start(f32[16,52,8,128]{3,2,1,0:T(8,128)} %bitcast.180), calls=%async_computation | async-start | bytes 6815744 | tf_op jit(solution)/shard_map/cond/branch_0_fun/all_to_all | solution.py:645
  467.6 48.6 %branch_0_fun.2.partial_ref = f32[4096,2048]{1,0:T(8,128)} custom-call(s32[32,82]{1,0:T(8,128)S(1)} %get-tuple-element.85.code_ref, s32[32,82]{1,0:T(8,128)} %copy.134.run_ref, s32[2]{0:T(128)S(1)} %copy-done.23, f32[4096,2048]{1,0:T(8,128)} %get-tuple-element.88.front_ref, f32[4096,256]{1,0:T(8,128)} %get-tuple-element.89.rows_ref, ...), custom_call_target="tpu_custom_call" | custom-call | tf_op jit(solution)/shard_map/cond/branch_0_fun/pallas_call | solution.py:425
  516.2 2.4 all-to-all-done
  518.5 10.6 %branch_0_fun.3 = f32[4096,2048]{1,0:T(8,128)} custom-call(s32[832]{0:T(1024)S(1)} %get-tuple-element.81.block_ref, s32[832]{0:T(1024)S(1)} %get-tuple-element.82.unit_ref, s32[832]{0:T(1024)S(1)} %get-tuple-element.83.index_ref, s32[1]{0:T(128)} %get-tuple-element.84.count_ref, ...), custom_call_target="tpu_custom_call", output_to_operand_aliasing={{}: (4, {})} | custom-call | tf_op jit(solution)/shard_map/cond/branch_0_fun/pallas_call | solution.py:234
  (166 shorter events, 34.9 us)
Async XLA Ops:
  6.5 179.3 %reduce-scatter.5.cloned.1.call-start = ((), (), s32[]{:S(2)}) async-start(), calls=%async_computation.10 | async-start | bytes 4718592 | tf_op jit(solution)/shard_map/reduce_scatter | solution.py:515
  7.4 9.0 %copy-start.16 = (s32[32,128]{1,0:T(8,128)}, s32[32,128]{1,0:T(8,128)S(1)}, u32[]{:S(2)}) copy-start(s32[32,128]{1,0:T(8,128)S(1)} %get-tuple-element.281) | copy-start | bytes 49156
  7.5 181.0 %copy-start.22 = (pred[32,128]{1,0:T(8,128)(4,1)}, pred[32,128]{1,0:T(8,128)(4,1)S(1)}, u32[]{:S(2)}) copy-start(pred[32,128]{1,0:T(8,128)(4,1)S(1)} %get-tuple-element.249) | copy-start | bytes 12292
  16.4 4.2 copy-start.20
  16.5 32.4 %collective-permute-start.12 = (f32[5,128,128]{2,1,0:T(8,128)S(1)}, f32[5,128,128]{2,1,0:T(8,128)S(1)}, u32[]{:S(2)}, u32[]{:S(2)}) collective-permute-start(f32[5,128,128]{2,1,0:T(8,128)S(1)} %get-tuple-element.267), channel_id=1, source_target_pairs={{0,24},{8,0},{16,8},{24,16},{1,25},{9,1},{17,9},{25,17},{2,26},{10... | collective-permute-start | bytes 983048 | tf_op jit(solution)/shard_map/ppermute | solution.py:502
  19.8 29.1 %collective-permute-start.11 = (f32[5,128,128]{2,1,0:T(8,128)S(1)}, f32[5,128,128]{2,1,0:T(8,128)S(1)}, u32[]{:S(2)}, u32[]{:S(2)}) collective-permute-start(f32[5,128,128]{2,1,0:T(8,128)S(1)} %get-tuple-element.268), channel_id=1, source_target_pairs={{0,16},{8,24},{16,0},{24,8},{1,17},{9,25},{17,1},{25,9},{2,18},{10... | collective-permute-start | bytes 983048 | tf_op jit(solution)/shard_map/ppermute | solution.py:502
  19.8 29.1 %collective-permute-start.10 = (f32[5,128,128]{2,1,0:T(8,128)S(1)}, f32[5,128,128]{2,1,0:T(8,128)S(1)}, u32[]{:S(2)}, u32[]{:S(2)}) collective-permute-start(f32[5,128,128]{2,1,0:T(8,128)S(1)} %get-tuple-element.269), channel_id=1, source_target_pairs={{0,8},{8,16},{16,24},{24,0},{1,9},{9,17},{17,25},{25,1},{2,10},{10... | collective-permute-start | bytes 983048 | tf_op jit(solution)/shard_map/ppermute | solution.py:502
  21.2 23.5 %copy-start.14 = (s32[3,4,1,128]{3,2,1,0:T(1,128)}, s32[3,4,1,128]{3,2,1,0:T(1,128)S(1)}, u32[]{:S(2)}) copy-start(s32[3,4,1,128]{3,2,1,0:T(1,128)S(1)} %fusion.81) | copy-start | bytes 18436
  44.7 4.2 copy-start.3
  52.0 1.9 copy-start.1
  64.6 356.3 %all-to-all-start.3 = ((f32[32,82,8,128]{3,2,1,0:T(8,128)}), f32[32,82,8,128]{3,2,1,0:T(8,128)}, u32[]{:S(2)}, u32[]{:S(2)}) async-start(f32[32,82,8,128]{3,2,1,0:T(8,128)} %copy-done.3), calls=%async_computation.4 | async-start | bytes 21495808 | tf_op jit(solution)/shard_map/all_to_all | solution.py:565
  70.6 215.3 %all-gather.13.cloned.1.call-start = ((), (), s32[]{:S(2)}) async-start(), calls=%async_computation.12 | async-start | bytes 2621440 | tf_op jit(solution)/shard_map/all_gather | solution.py:516
  185.9 157.5 %all-gather.11.cloned.1.call-start = ((), (), s32[]{:S(2)}) async-start(), calls=%async_computation.11 | async-start | bytes 4718592 | tf_op jit(solution)/shard_map/all_gather | solution.py:517
  392.9 7.1 %collective-permute-start.14 = (f32[256,256]{1,0:T(8,128)S(1)}, f32[256,256]{1,0:T(8,128)S(1)}, u32[]{:S(2)}, u32[]{:S(2)}) collective-permute-start(f32[256,256]{1,0:T(8,128)S(1)} %fusion.38), channel_id=1, source_target_pairs={{0,16},{1,17},{2,18},{3,19},{4,20},{5,21},{6,22},{7,23}} | collective-permute-start | bytes 786440 | tf_op jit(solution)/shard_map/ppermute | solution.py:633
  394.2 11.4 %collective-permute-start.15 = (f32[256,256]{1,0:T(8,128)S(1)}, f32[256,256]{1,0:T(8,128)S(1)}, u32[]{:S(2)}, u32[]{:S(2)}) collective-permute-start(f32[256,256]{1,0:T(8,128)S(1)} %fusion.38), channel_id=1, source_target_pairs={{0,24},{1,25},{2,26},{3,27},{4,28},{5,29},{6,30},{7,31}} | collective-permute-start | bytes 786440 | tf_op jit(solution)/shard_map/ppermute | solution.py:633
  397.8 13.4 %collective-permute-start.13 = (f32[256,256]{1,0:T(8,128)S(1)}, f32[256,256]{1,0:T(8,128)S(1)}, u32[]{:S(2)}, u32[]{:S(2)}) collective-permute-start(f32[256,256]{1,0:T(8,128)S(1)} %fusion.38), channel_id=1, source_target_pairs={{0,8},{1,9},{2,10},{3,11},{4,12},{5,13},{6,14},{7,15}} | collective-permute-start | bytes 786440 | tf_op jit(solution)/shard_map/ppermute | solution.py:633
  411.2 2.2 copy-start.5
  413.4 14.1 %copy-start.10 = (f32[2048,256]{1,0:T(8,128)S(1)}, f32[2048,256]{1,0:T(8,128)}, u32[]{:S(2)}) copy-start(f32[2048,256]{1,0:T(8,128)} %all-gather.13.cloned.1.call-done) | copy-start | bytes 6291460
  420.9 28.1 %all-to-all-start.4 = ((s32[32,1,53]{2,1,0:T(1,128)}), s32[32,1,53]{2,1,0:T(1,128)S(1)}, u32[]{:S(2)}, u32[]{:S(2)}) async-start(s32[32,1,53]{2,1,0:T(1,128)} %bitcast.54), calls=%async_computation.5 | async-start | bytes 32768 | tf_op jit(solution)/shard_map/all_to_all | solution.py:593
  428.7 25.4 %collective-permute-start.16 = (f32[512,256]{1,0:T(8,128)}, f32[512,256]{1,0:T(8,128)S(1)}, u32[]{:S(2)}, u32[]{:S(2)}) collective-permute-start(f32[512,256]{1,0:T(8,128)} %get-tuple-element.262), channel_id=1, source_target_pairs={{0,0},{1,2},{2,4},{3,6},{4,1},{5,3},{6,5},{7,7},{8,8},{9,10},{10,1... | collective-permute-start | bytes 1572872 | tf_op jit(solution)/shard_map/ppermute | solution.py:629
  430.3 23.7 %collective-permute-start.19 = (f32[512,256]{1,0:T(8,128)}, f32[512,256]{1,0:T(8,128)S(1)}, u32[]{:S(2)}, u32[]{:S(2)}) collective-permute-start(f32[512,256]{1,0:T(8,128)} %get-tuple-element.263), channel_id=1, source_target_pairs={{0,6},{1,0},{2,2},{3,4},{4,7},{5,1},{6,3},{7,5},{8,14},{9,8},{10,1... | collective-permute-start | bytes 1572872 | tf_op jit(solution)/shard_map/ppermute | solution.py:629
  433.9 20.1 %collective-permute-start.18 = (f32[512,256]{1,0:T(8,128)S(1)}, f32[512,256]{1,0:T(8,128)S(1)}, u32[]{:S(2)}, u32[]{:S(2)}) collective-permute-start(f32[512,256]{1,0:T(8,128)S(1)} %get-tuple-element.264), channel_id=1, source_target_pairs={{0,4},{1,6},{2,0},{3,2},{4,5},{5,7},{6,1},{7,3},{8,12},{9,14},{10,... | collective-permute-start | bytes 1572872 | tf_op jit(solution)/shard_map/ppermute | solution.py:629
  434.4 20.2 %collective-permute-start.17 = (f32[512,256]{1,0:T(8,128)S(1)}, f32[512,256]{1,0:T(8,128)S(1)}, u32[]{:S(2)}, u32[]{:S(2)}) collective-permute-start(f32[512,256]{1,0:T(8,128)S(1)} %get-tuple-element.265), channel_id=1, source_target_pairs={{0,2},{1,4},{2,6},{3,0},{4,3},{5,5},{6,7},{7,1},{8,10},{9,12},{10,... | collective-permute-start | bytes 1572872 | tf_op jit(solution)/shard_map/ppermute | solution.py:629
  454.7 4.8 copy-start.13
  454.7 4.8 copy-start.15
  454.7 4.8 copy-start.17
  454.8 4.8 copy-start.18
  454.8 4.8 copy-start.19
  459.6 8.0 %copy-start.23 = (s32[2]{0:T(128)S(1)}, s32[2]{0:T(128)}, u32[]{:S(2)}) copy-start(s32[2]{0:T(128)} %get-tuple-element.87.place_ref) | copy-start | bytes 28 | tf_op jit(solution)/shard_map/cond
  459.6 58.9 %all-to-all-start = ((f32[16,52,8,128]{3,2,1,0:T(8,128)}), f32[16,52,8,128]{3,2,1,0:T(8,128)S(1)}, u32[]{:S(2)}, u32[]{:S(2)}) async-start(f32[16,52,8,128]{3,2,1,0:T(8,128)} %bitcast.180), calls=%async_computation | async-start | bytes 6815744 | tf_op jit(solution)/shard_map/cond/branch_0_fun/all_to_all | solution.py:645
Sparse Core Ops, SparseCore 0:
  54.1 131.7 reduce-scatter.4
  187.4 98.4 all-gather.12
  287.8 55.4 all-gather.10

commit v2 on v1

--- a/solution.py
+++ b/solution.py
@@ -513,8 +513,9 @@
 
     def gather_panel(partial):
         chunk = lax.psum_scatter(partial, "col", scatter_dimension=0, tiled=True)
-        gathered = lax.all_gather(chunk, "row", axis=0)
-        return gathered, lax.all_gather(chunk, "col", axis=0, tiled=True)
+        raw_rows = lax.all_gather(chunk, "col", axis=0, tiled=True)
+        chunk, raw_rows = lax.optimization_barrier((chunk, raw_rows))
+        return lax.all_gather(chunk, "row", axis=0), raw_rows
 
     panel_depth = (capacity * 5 + 7) // 8
     panel_in = send_panel(tiles, valid_rows, panel_depth)
@@ -612,11 +613,10 @@
 
     passed = relay(relay_slot, arrived, half_count * pass_on)
     def chain(gathered, raw_rows, arrived):
-        gathered, raw_rows = lax.optimization_barrier((gathered, raw_rows))
         diagonal = jnp.where(row_now == 0, raw_rows[:TOTAL], jnp.eye(TOTAL, dtype=jnp.float32))
         lower, inverse = factor(diagonal)
         known = jnp.where(row_now == 0, inverse, 0.0)
-        gathered, arrived = lax.optimization_barrier((gathered, arrived))
+        gathered, known, arrived = lax.optimization_barrier((gathered, known, arrived))
         share = col_count // row_count
         chunks = []
         for turn in range(row_count):

time: 545 us -> 487 us (0.89)
  waiting for transfers between devices: 268 us -> 198 us
    all_gather x2, waiting for transfers between devices: 138 us -> 36 us  [the longest x1 36 us: gather_panel(): raw_rows = lax.all_gather(chunk, 'col', axis=0, tiled=True)]
    all_to_all x1, waiting for transfers between devices: 0.01 us -> 34.4 us  [body(): arrived = lax.all_to_all(outgoing, ('row', 'col'), 0, 0, tiled=True)]
    ppermute x3, waiting for transfers between devices: 11.2 us -> 0.01 us  [chain(): inverse += lax.ppermute(known, 'row', [(0, other)])]
    reduce_scatter x1, waiting for transfers between devices: 115 us -> 126 us  [gather_panel(): chunk = lax.psum_scatter(partial, 'col', scatter_dimension=0, tiled=True)]
  transfers between devices with their start and end apart: 16 -> 16, of which waited for: 7 -> 4; matrix products, arithmetic and copies ran while one was open for 14% -> 17% of each run, Pallas kernels for 16% -> 18%
where the time goes in v2:
time: 487 us; the launch traced here: 479 us
  waiting for transfers between devices  198 us (41%)
  Pallas kernels  112 us (23%)
  other arithmetic  71.2 us (15%)
  starting transfers between devices  45.8 us (9%)
  local copies, waits for them, and re-layouts  21.9 us (4%)
  between operations  16.7 us (3%)
  blocking collectives  10.9 us (2%)
    reduce_scatter x1, waiting for transfers between devices, gather_panel(): chunk = lax.psum_scatter(partial, 'col', scatter_dimension=0, tiled=True)  126 us
    pallas_call x1, Pallas kernels, finish(): pl.pallas_call(functools.partial(final_kernel, cols_blocks, runs), grid=(...  50 us
    all_gather x1, waiting for transfers between devices, gather_panel(): raw_rows = lax.all_gather(chunk, 'col', axis=0, tiled=True)  36 us
    all_to_all x1, waiting for transfers between devices, body(): arrived = lax.all_to_all(outgoing, ('row', 'col'), 0, 0, tiled=True)  34.4 us
    another operation x6, other arithmetic, lower_of(): return jnp.linalg.cholesky(jnp.tril(block) + jnp.tril(block, -1).T)  25.2 us
    another operation x5, other arithmetic, inverse_of(): jax.scipy.linalg.solve_triangular(block, jnp.eye(NB, dtype=jnp.float32),...  20.9 us
    pallas_call x1, Pallas kernels, spread(): pl.pallas_call(functools.partial(spread_kernel, width, stride), out_shape...  20.8 us
    pallas_call x1, Pallas kernels, add_relayed(): pl.pallas_call(functools.partial(add_kernel, cols_blocks), out_shape=jax....  10.9 us
  transfers between devices with their start and end apart: 16, of which 4 were waited for; matrix products, arithmetic and copies ran while one was open for 17% of the time, Pallas kernels for 18%

profile of v2, /device:TPU:7, one launch (start us, length us, event | category | flops | bytes accessed | tf_op | source)
XLA Modules:
  0.0 478.6 jit_solution(10073255458577220124)
XLA Ops:
  9.4 7.1 %shard_map.49 = f32[20,128,128]{2,1,0:T(8,128)S(1)} custom-call(s32[128]{0:T(128)S(1)} %get-tuple-element.291.slot_ref, s32[128]{0:T(128)} %valid_ref.1, f32[128,128,128]{2,1,0:T(8,128)} %tiles_ref.1), custom_call_target="tpu_custom_call" | custom-call | tf_op jit(solution)/shard_map/pallas_call | solution.py:56
  16.6 3.4 collective-permute-start.12
  23.5 20.8 %shard_map.48 = (f32[32,82,8,128]{3,2,1,0:T(8,128)S(1)}, s32[32,128]{1,0:T(8,128)S(1)}) custom-call(s32[6,128]{1,0:T(8,128)S(1)} %select_reduce_fusion.7.meta_ref, s32[2,16]{1,0:T(2,128)S(1)} %select_reduce_fusion.11.empty_ref, s32[3]{0:T(128)S(1)} %pad_add_fusion.1.count_ref, f32[128,16,8,128]{3,2,1,0:T(8,128)} %bitcast.179), custom_call_target="tpu_custom_call" | custom-call | tf_op jit(solution)/shard_map/pallas_call | solution.py:122
  44.3 4.2 copy-done.3
  48.6 3.0 shard_map.50
  51.5 1.9 copy-done.1
  53.5 10.9 %all_to_all.37 = s32[32,1,82]{2,1,0:T(1,128)S(1)} all-to-all(s32[32,1,82]{2,1,0:T(1,128)S(1)} %bitcast.178), channel_id=1, replica_groups=mesh['row'=4,'col'=8] {'row','col'}, dimensions={0} | all-to-all | bytes 20992 | tf_op jit(solution)/shard_map/all_to_all | solution.py:564
  64.3 6.0 %all-to-all-start.3 = ((f32[32,82,8,128]{3,2,1,0:T(8,128)}), f32[32,82,8,128]{3,2,1,0:T(8,128)}, u32[]{:S(2)}, u32[]{:S(2)}) async-start(f32[32,82,8,128]{3,2,1,0:T(8,128)} %copy-done.3), calls=%async_computation.4 | async-start | bytes 21495808 | tf_op jit(solution)/shard_map/all_to_all | solution.py:566
  71.1 125.7 %reduce-scatter.5.cloned.1.call-done = f32[512,256]{1,0:T(8,128)} async-done(((f32[4096,256]{1,0:T(8,128)}), f32[512,256]{1,0:T(8,128)}) %reduce-scatter.5.cloned.1.call-update) | async-done | bytes 524304 | tf_op jit(solution)/shard_map/reduce_scatter | solution.py:515
  202.5 6.1 %convert_reduce_fusion.1 = s32[2624]{0:T(1024)S(1)} fusion(s32[2624]{0:T(1024)S(1)} %get-tuple-element.290, s32[2624]{0:T(1024)S(1)} %get-tuple-element.289), kind=kLoop, calls=%fused_computation.109 | loop fusion | flops 34424256 | bytes 31488 | tf_op jit(solution)/shard_map/reduce_sum | solution.py:579
  216.1 36.0 %all-gather.11.cloned.1.call-done.raw_ref = f32[4096,256]{1,0:T(8,128)} async-done(((f32[512,256]{1,0:T(8,128)}), f32[4096,256]{1,0:T(8,128)}) %all-gather.11.cloned.1.call-update) | async-done | bytes 4194320 | tf_op jit(solution)/shard_map/all_gather | solution.py:516
  253.5 11.7 %cholesky.96 = f32[128,128]{1,0:T(8,128)S(1)} custom-call(f32[128,128]{1,0:T(8,128)S(1)} %copy.125), custom_call_target="Cholesky" | custom-call | tf_op jit(solution)/shard_map/jit(cholesky)/cholesky | solution.py:442
  266.5 9.8 %custom-call.10 = f32[1,128,128]{1,2,0:T(8,128)S(1)} custom-call(f32[1,128,128]{2,1,0:T(8,128)S(1)} %get-tuple-element.249), custom_call_target="InvertDiagBlocksLowerTriangular" | custom-call | tf_op jit(solution)/shard_map/jit(_solve_triangular)/triangular_solve | solution.py:445
  277.6 12.1 %cholesky.107 = f32[128,128]{1,0:T(8,128)S(1)} custom-call(f32[128,128]{1,0:T(8,128)S(1)} %fusion.47), custom_call_target="Cholesky" | custom-call | tf_op jit(solution)/shard_map/jit(cholesky)/cholesky | solution.py:442
  291.0 9.8 %custom-call.11 = f32[1,128,128]{1,2,0:T(8,128)S(1)} custom-call(f32[1,128,128]{2,1,0:T(8,128)S(1)} %get-tuple-element.247), custom_call_target="InvertDiagBlocksLowerTriangular" | custom-call | tf_op jit(solution)/shard_map/jit(_solve_triangular)/triangular_solve | solution.py:445
  303.2 34.4 %all-to-all-done.3.arrived_ref = f32[32,82,8,128]{3,2,1,0:T(8,128)} async-done(((f32[32,82,8,128]{3,2,1,0:T(8,128)}), f32[32,82,8,128]{3,2,1,0:T(8,128)}, u32[]{:S(2)}, u32[]{:S(2)}) %all-to-all-start.3) | async-done | bytes 10747936 | tf_op jit(solution)/shard_map/all_to_all | solution.py:566
  337.6 4.6 collective-permute-start.15
  342.3 2.0 collective-permute-start.14
  344.2 2.0 collective-permute-start.13
  346.2 8.6 %all-to-all-start.4 = ((s32[32,1,53]{2,1,0:T(1,128)}), s32[32,1,53]{2,1,0:T(1,128)S(1)}, u32[]{:S(2)}, u32[]{:S(2)}) async-start(s32[32,1,53]{2,1,0:T(1,128)} %bitcast.54), calls=%async_computation.5 | async-start | bytes 32768 | tf_op jit(solution)/shard_map/all_to_all | solution.py:594
  354.8 2.9 dynamic-slice_bitcast_fusion.7
  357.7 5.3 %collective-permute-start.16 = (f32[512,256]{1,0:T(8,128)}, f32[512,256]{1,0:T(8,128)}, u32[]{:S(2)}, u32[]{:S(2)}) collective-permute-start(f32[512,256]{1,0:T(8,128)} %get-tuple-element.265), channel_id=1, source_target_pairs={{0,0},{1,2},{2,4},{3,6},{4,1},{5,3},{6,5},{7,7},{8,8},{9,10},{10,1... | collective-permute-start | bytes 1572872 | tf_op jit(solution)/shard_map/ppermute | solution.py:629
  363.1 1.9 collective-permute-start.19
  365.0 7.4 %shard_map.53 = f32[832,8,128]{2,1,0:T(8,128)S(1)} custom-call(s32[32,82]{1,0:T(8,128)S(1)} %add_select_fusion.13.slot_ref, f32[32,82,8,128]{3,2,1,0:T(8,128)} %all-to-all-done.3.arrived_ref), custom_call_target="tpu_custom_call" | custom-call | tf_op jit(solution)/shard_map/pallas_call | solution.py:155
  374.5 3.2 collective-permute-start.17
  382.0 2.2 copy-done.5
  384.2 7.5 %shard_map.51 = (f32[4096,256]{1,0:T(8,128)}, bf16[4096,768]{1,0:T(8,128)(2,1)}) custom-call(f32[4096,256]{1,0:T(8,128)S(1)} %copy-done.5, f32[256,256]{1,0:T(8,128)S(1)} %add_add_fusion.1.inverse_ref), custom_call_target="tpu_custom_call" | custom-call | tf_op jit(solution)/shard_map/pallas_call | solution.py:309
  393.4 4.9 %shard_map.52 = (f32[256,2048]{1,0:T(8,128)}, bf16[768,2048]{1,0:T(8,128)(2,1)}) custom-call(s32[4]{0:T(128)S(1)} %and_select_fusion.8.order_ref, f32[4,512,256]{2,1,0:T(8,128)S(1)} %pad_maximum_fusion.2.raw_ref, f32[256,256]{1,0:T(8,128)S(1)} %add_add_fusion.1.inverse_ref), custom_call_target="tpu_custom_call" | custom-call | tf_op jit(solution)/shard_map/pallas_call | solution.py:346
  398.2 73.6 %conditional.1 = (f32[4096,2048]{1,0:T(8,128)}) conditional(s32[]{:T(128)} %convert_element_type.63, (s32[32,82]{1,0:T(8,128)S(1)}, s32[32,82]{0,1:T(8,128)S(1)}, s32[2]{0:T(128)}, f32[4096,2048]{1,0:T(8,128)}, f32[4096,256]{1,0:T(8,128)}, /*index=5*/bf16[4096,768]{1,0:T(8,128)(2,1)}, f32[256,2048]{1,0:T(8,128)}, bf16[768,2048]{1,0:T(8,128)(2,1)}, ...), branch_computations={%region_24.27_spmd, %region_25.32_spmd} | conditional | flops 158485968 | bytes 293366400 | solution.py:673
  400.0 8.3 %all-to-all-start = ((f32[16,52,8,128]{3,2,1,0:T(8,128)}), f32[16,52,8,128]{3,2,1,0:T(8,128)S(1)}, u32[]{:S(2)}, u32[]{:S(2)}) async-start(f32[16,52,8,128]{3,2,1,0:T(8,128)} %bitcast.180), calls=%async_computation | async-start | bytes 6815744 | tf_op jit(solution)/shard_map/cond/branch_0_fun/all_to_all | solution.py:645
  408.9 50.0 %branch_0_fun.2.partial_ref = f32[4096,2048]{1,0:T(8,128)} custom-call(s32[32,82]{1,0:T(8,128)S(1)} %get-tuple-element.85.code_ref, s32[32,82]{1,0:T(8,128)} %copy.134.run_ref, s32[2]{0:T(128)S(1)} %copy-done.19, f32[4096,2048]{1,0:T(8,128)} %get-tuple-element.88.front_ref, f32[4096,256]{1,0:T(8,128)} %get-tuple-element.89.rows_ref, ...), custom_call_target="tpu_custom_call" | custom-call | tf_op jit(solution)/shard_map/cond/branch_0_fun/pallas_call | solution.py:425
  459.9 10.9 %branch_0_fun.3 = f32[4096,2048]{1,0:T(8,128)} custom-call(s32[832]{0:T(1024)S(1)} %copy-done.15, s32[832]{0:T(1024)S(1)} %get-tuple-element.82.unit_ref, s32[832]{0:T(1024)S(1)} %get-tuple-element.83.index_ref, s32[1]{0:T(128)} %get-tuple-element.84.count_ref, f32[4096,2048]{1,0:T(8,128)} %branch_0_fun.2.partial_ref, ...), custom_call_target="tpu_custom_call", output_to_operand_aliasing={{}: (4, {})} | custom-call | tf_op jit(solution)/shard_map/cond/branch_0_fun/pallas_call | solution.py:234
  (158 shorter events, 36.3 us)
Async XLA Ops:
  7.4 9.1 %copy-start.14 = (s32[32,128]{1,0:T(8,128)}, s32[32,128]{1,0:T(8,128)S(1)}, u32[]{:S(2)}) copy-start(s32[32,128]{1,0:T(8,128)S(1)} %get-tuple-element.284) | copy-start | bytes 49156
  7.5 191.3 %copy-start.18 = (pred[32,128]{1,0:T(8,128)(4,1)}, pred[32,128]{1,0:T(8,128)(4,1)S(1)}, u32[]{:S(2)}) copy-start(pred[32,128]{1,0:T(8,128)(4,1)S(1)} %get-tuple-element.252) | copy-start | bytes 12292
  16.5 3.8 copy-start.16
  16.6 31.8 %collective-permute-start.12 = (f32[5,128,128]{2,1,0:T(8,128)S(1)}, f32[5,128,128]{2,1,0:T(8,128)S(1)}, u32[]{:S(2)}, u32[]{:S(2)}) collective-permute-start(f32[5,128,128]{2,1,0:T(8,128)S(1)} %get-tuple-element.270), channel_id=1, source_target_pairs={{0,24},{8,0},{16,8},{24,16},{1,25},{9,1},{17,9},{25,17},{2,26},{10... | collective-permute-start | bytes 983048 | tf_op jit(solution)/shard_map/ppermute | solution.py:502
  20.0 28.4 %collective-permute-start.11 = (f32[5,128,128]{2,1,0:T(8,128)S(1)}, f32[5,128,128]{2,1,0:T(8,128)S(1)}, u32[]{:S(2)}, u32[]{:S(2)}) collective-permute-start(f32[5,128,128]{2,1,0:T(8,128)S(1)} %get-tuple-element.271), channel_id=1, source_target_pairs={{0,16},{8,24},{16,0},{24,8},{1,17},{9,25},{17,1},{25,9},{2,18},{10... | collective-permute-start | bytes 983048 | tf_op jit(solution)/shard_map/ppermute | solution.py:502
  20.0 28.4 %collective-permute-start.10 = (f32[5,128,128]{2,1,0:T(8,128)S(1)}, f32[5,128,128]{2,1,0:T(8,128)S(1)}, u32[]{:S(2)}, u32[]{:S(2)}) collective-permute-start(f32[5,128,128]{2,1,0:T(8,128)S(1)} %get-tuple-element.272), channel_id=1, source_target_pairs={{0,8},{8,16},{16,24},{24,0},{1,9},{9,17},{17,25},{25,1},{2,10},{10... | collective-permute-start | bytes 983048 | tf_op jit(solution)/shard_map/ppermute | solution.py:502
  44.3 4.2 copy-start.3
  51.5 1.9 copy-start.1
  64.3 273.3 %all-to-all-start.3 = ((f32[32,82,8,128]{3,2,1,0:T(8,128)}), f32[32,82,8,128]{3,2,1,0:T(8,128)}, u32[]{:S(2)}, u32[]{:S(2)}) async-start(f32[32,82,8,128]{3,2,1,0:T(8,128)} %copy-done.3), calls=%async_computation.4 | async-start | bytes 21495808 | tf_op jit(solution)/shard_map/all_to_all | solution.py:566
  70.3 126.5 %reduce-scatter.5.cloned.1.call-start = ((), (), s32[]{:S(2)}) async-start(), calls=%async_computation.10 | async-start | bytes 4718592 | tf_op jit(solution)/shard_map/reduce_scatter | solution.py:515
  71.1 181.1 %all-gather.11.cloned.1.call-start = ((), (), s32[]{:S(2)}) async-start(), calls=%async_computation.11 | async-start | bytes 4718592 | tf_op jit(solution)/shard_map/all_gather | solution.py:516
  196.8 140.8 %all-gather.13.cloned.1.call-start = ((), (), s32[]{:S(2)}) async-start(), calls=%async_computation.12 | async-start | bytes 2621440 | tf_op jit(solution)/shard_map/all_gather | solution.py:518
  337.6 36.8 %collective-permute-start.15 = (f32[256,256]{1,0:T(8,128)}, f32[256,256]{1,0:T(8,128)}, u32[]{:S(2)}, u32[]{:S(2)}) collective-permute-start(f32[256,256]{1,0:T(8,128)} %fusion.38), channel_id=1, source_target_pairs={{0,24},{1,25},{2,26},{3,27},{4,28},{5,29},{6,30},{7,31}} | collective-permute-start | bytes 786440 | tf_op jit(solution)/shard_map/ppermute | solution.py:633
  342.3 32.2 %collective-permute-start.14 = (f32[256,256]{1,0:T(8,128)}, f32[256,256]{1,0:T(8,128)}, u32[]{:S(2)}, u32[]{:S(2)}) collective-permute-start(f32[256,256]{1,0:T(8,128)} %fusion.38), channel_id=1, source_target_pairs={{0,16},{1,17},{2,18},{3,19},{4,20},{5,21},{6,22},{7,23}} | collective-permute-start | bytes 786440 | tf_op jit(solution)/shard_map/ppermute | solution.py:633
  344.2 36.5 %collective-permute-start.13 = (f32[256,256]{1,0:T(8,128)}, f32[256,256]{1,0:T(8,128)}, u32[]{:S(2)}, u32[]{:S(2)}) collective-permute-start(f32[256,256]{1,0:T(8,128)} %fusion.38), channel_id=1, source_target_pairs={{0,8},{1,9},{2,10},{3,11},{4,12},{5,13},{6,14},{7,15}} | collective-permute-start | bytes 786440 | tf_op jit(solution)/shard_map/ppermute | solution.py:633
  346.2 26.2 %all-to-all-start.4 = ((s32[32,1,53]{2,1,0:T(1,128)}), s32[32,1,53]{2,1,0:T(1,128)S(1)}, u32[]{:S(2)}, u32[]{:S(2)}) async-start(s32[32,1,53]{2,1,0:T(1,128)} %bitcast.54), calls=%async_computation.5 | async-start | bytes 32768 | tf_op jit(solution)/shard_map/all_to_all | solution.py:594
  357.7 34.0 %collective-permute-start.16 = (f32[512,256]{1,0:T(8,128)}, f32[512,256]{1,0:T(8,128)}, u32[]{:S(2)}, u32[]{:S(2)}) collective-permute-start(f32[512,256]{1,0:T(8,128)} %get-tuple-element.265), channel_id=1, source_target_pairs={{0,0},{1,2},{2,4},{3,6},{4,1},{5,3},{6,5},{7,7},{8,8},{9,10},{10,1... | collective-permute-start | bytes 1572872 | tf_op jit(solution)/shard_map/ppermute | solution.py:629
  363.1 28.6 %collective-permute-start.19 = (f32[512,256]{1,0:T(8,128)}, f32[512,256]{1,0:T(8,128)}, u32[]{:S(2)}, u32[]{:S(2)}) collective-permute-start(f32[512,256]{1,0:T(8,128)} %get-tuple-element.266), channel_id=1, source_target_pairs={{0,6},{1,0},{2,2},{3,4},{4,7},{5,1},{6,3},{7,5},{8,14},{9,8},{10,1... | collective-permute-start | bytes 1572872 | tf_op jit(solution)/shard_map/ppermute | solution.py:629
  374.4 17.3 %collective-permute-start.18 = (f32[512,256]{1,0:T(8,128)}, f32[512,256]{1,0:T(8,128)}, u32[]{:S(2)}, u32[]{:S(2)}) collective-permute-start(f32[512,256]{1,0:T(8,128)} %get-tuple-element.267), channel_id=1, source_target_pairs={{0,4},{1,6},{2,0},{3,2},{4,5},{5,7},{6,1},{7,3},{8,12},{9,14},{10,... | collective-permute-start | bytes 1572872 | tf_op jit(solution)/shard_map/ppermute | solution.py:629
  374.5 17.2 %collective-permute-start.17 = (f32[512,256]{1,0:T(8,128)}, f32[512,256]{1,0:T(8,128)}, u32[]{:S(2)}, u32[]{:S(2)}) collective-permute-start(f32[512,256]{1,0:T(8,128)} %get-tuple-element.268), channel_id=1, source_target_pairs={{0,2},{1,4},{2,6},{3,0},{4,3},{5,5},{6,7},{7,1},{8,10},{9,12},{10,... | collective-permute-start | bytes 1572872 | tf_op jit(solution)/shard_map/ppermute | solution.py:629
  382.0 2.2 copy-start.5
  393.4 4.9 %copy-start.13 = (s32[32,82]{1,0:T(8,128)S(1)}, s32[32,82]{1,0:T(8,128)}, u32[]{:S(2)}) copy-start(s32[32,82]{1,0:T(8,128)} %get-tuple-element.162) | copy-start | bytes 31492
  398.2 1.7 copy-start.10
  400.0 9.0 %copy-start.19 = (s32[2]{0:T(128)S(1)}, s32[2]{0:T(128)}, u32[]{:S(2)}) copy-start(s32[2]{0:T(128)} %get-tuple-element.87.place_ref) | copy-start | bytes 28 | tf_op jit(solution)/shard_map/cond
  400.0 59.9 %all-to-all-start = ((f32[16,52,8,128]{3,2,1,0:T(8,128)}), f32[16,52,8,128]{3,2,1,0:T(8,128)S(1)}, u32[]{:S(2)}, u32[]{:S(2)}) async-start(f32[16,52,8,128]{3,2,1,0:T(8,128)} %bitcast.180), calls=%async_computation | async-start | bytes 6815744 | tf_op jit(solution)/shard_map/cond/branch_0_fun/all_to_all | solution.py:645
  408.9 50.9 %copy-start.15 = (s32[832]{0:T(1024)S(1)}, s32[832]{0:T(1024)}, u32[]{:S(2)}) copy-start(s32[832]{0:T(1024)} %get-tuple-element.81.block_ref) | copy-start | bytes 9988 | tf_op jit(solution)/shard_map/cond
Sparse Core Ops, SparseCore 0:
  74.9 121.8 reduce-scatter.4
  198.7 53.3 all-gather.10
  253.7 68.8 all-gather.12

commit v3 on v2

--- a/solution.py
+++ b/solution.py
@@ -594,7 +594,6 @@
     notes = lax.all_to_all(
         notes.reshape(device_count, pass_on + 1), ("row", "col"), 0, 0, tiled=True
     )
-    too_full = jnp.any(notes[:, pass_on] != 0)
     relay_codes = lax.dynamic_slice_in_dim(notes, half_base, half_count, 0)[:, :pass_on]
     relay_slot = relay_slot.reshape(device_count, width)
 
@@ -612,11 +611,11 @@
     listing = [*listing, jnp.sum(wanted).astype(jnp.int32).reshape(1)]
 
     passed = relay(relay_slot, arrived, half_count * pass_on)
-    def chain(gathered, raw_rows, arrived):
+    def chain(gathered, raw_rows):
         diagonal = jnp.where(row_now == 0, raw_rows[:TOTAL], jnp.eye(TOTAL, dtype=jnp.float32))
         lower, inverse = factor(diagonal)
         known = jnp.where(row_now == 0, inverse, 0.0)
-        gathered, known, arrived = lax.optimization_barrier((gathered, known, arrived))
+        gathered, known = lax.optimization_barrier((gathered, known))
         share = col_count // row_count
         chunks = []
         for turn in range(row_count):
@@ -635,23 +634,18 @@
         cols = solve_cols(jnp.stack(chunks), order.astype(jnp.int32), inverse)
         return rows, cols, lower
 
-    tables = (direct_codes, direct_runs, listing)
-    rows, cols, lower = chain(gathered, raw_rows, arrived)
-    rows, cols, lower, passed, tables = lax.optimization_barrier((rows, cols, lower, passed, tables))
-    direct_codes, direct_runs, listing = tables
-
-    def relayed(front, tiles, valid_rows, arrived, passed, rows, cols, lower):
-        halves = [list(range(half_count)), list(range(half_count, device_count))]
-        passed = lax.all_to_all(
-            passed.reshape(half_count, pass_on, UNIT, side), ("row", "col"), 0, 0,
-            axis_index_groups=halves, tiled=True,
-        )
-        partial = finish(
-            front, rows, cols, lower, arrived, direct_codes, direct_runs, place, cols_blocks
-        )
-        return add_relayed(partial, passed.reshape(-1, UNIT, side), listing, cols_blocks)
-
-    def padded(front, tiles, valid_rows, arrived, passed, rows, cols, lower):
+    rows, cols, lower = chain(gathered, raw_rows)
+    passed, notes = lax.optimization_barrier((passed, notes))
+    too_full = jnp.any(notes[:, pass_on] != 0)
+    halves = [list(range(half_count)), list(range(half_count, device_count))]
+    passed = lax.all_to_all(
+        passed.reshape(half_count, pass_on, UNIT, side), ("row", "col"), 0, 0,
+        axis_index_groups=halves, tiled=True,
+    )
+    partial = finish(front, rows, cols, lower, arrived, direct_codes, direct_runs, place, cols_blocks)
+    result = add_relayed(partial, passed.reshape(-1, UNIT, side), listing, cols_blocks)
+
+    def padded():
         partial = sum_panel(front, send_panel(tiles, valid_rows, capacity), capacity)
         gathered, raw_rows = gather_panel(partial)
         order = (target * rows_blocks * cols_blocks + code) * per_device + position
@@ -665,14 +659,18 @@
         arrived = lax.all_to_all(
             packed.reshape(device_count, capacity, side, side), ("row", "col"), 0, 0, tiled=True
         )
-        rows, cols, lower = chain(gathered, raw_rows, arrived)
+        rows, cols, lower = chain(gathered, raw_rows)
         return finish(
             front, rows, cols, lower, arrived, codes, jnp.ones_like(codes), place, cols_blocks
         )
 
-    return lax.cond(
-        too_full, padded, relayed, front, tiles, valid_rows, arrived, passed, rows, cols, lower
-    )
+    def unfinished(state):
+        return state[0] > 0
+
+    def redo(state):
+        return jnp.int32(0), padded()
+
+    return lax.while_loop(unfinished, redo, (too_full.astype(jnp.int32), result))[1]
 
 
 def solution(mesh):

time: 487 us -> 606 us (1.24)
  local copies, waits for them, and re-layouts: 21.9 us -> 69.4 us
  waiting for transfers between devices: 198 us -> 241 us
  other arithmetic: 71.2 us -> 91.9 us
    all_to_all x1, waiting for transfers between devices: 34.4 us -> 84.8 us  [body(): arrived = lax.all_to_all(outgoing, ('row', 'col'), 0, 0, tiled=True)]
    dynamic_slice x0 -> x5, local copies, waits for them, and re-layouts: none -> 14.4 us  [chain(): lax.dynamic_index_in_dim(gathered, (col_now + turn) % row_count, 0, keepd...]
    optimization_barrier x0 -> x2, local copies, waits for them, and re-layouts: none -> 11.7 us  [the longest x1 6.04 us: gather_panel(): chunk, raw_rows = lax.optimization_barrier((chunk, raw_rows))]
    unnamed x15 -> x39, local copies, waits for them, and re-layouts: 8.29 us -> 18.6 us
  transfers between devices with their start and end apart: 16 -> 16, of which waited for: 4 -> 3; matrix products, arithmetic and copies ran while one was open for 17% -> 24% of each run, Pallas kernels for 18% -> 15%
where the time goes in v3:
time: 606 us; the launch traced here: 598 us
  waiting for transfers between devices  241 us (40%)
  Pallas kernels  110 us (18%)
  other arithmetic  91.9 us (15%)
  local copies, waits for them, and re-layouts  69.4 us (11%)
  starting transfers between devices  49.8 us (8%)
  between operations  16.7 us (3%)
  blocking collectives  11.7 us (2%)
  matrix products  6.45 us (1%)
    reduce_scatter x1, waiting for transfers between devices, gather_panel(): chunk = lax.psum_scatter(partial, 'col', scatter_dimension=0, tiled=True)  121 us
    all_to_all x1, waiting for transfers between devices, body(): arrived = lax.all_to_all(outgoing, ('row', 'col'), 0, 0, tiled=True)  84.8 us
    pallas_call x1, Pallas kernels, finish(): pl.pallas_call(functools.partial(final_kernel, cols_blocks, runs), grid=(...  49.9 us
    all_gather x1, waiting for transfers between devices, gather_panel(): raw_rows = lax.all_gather(chunk, 'col', axis=0, tiled=True)  35.1 us
    another operation x6, other arithmetic, lower_of(): return jnp.linalg.cholesky(jnp.tril(block) + jnp.tril(block, -1).T)  28.5 us
    another operation x5, other arithmetic, inverse_of(): jax.scipy.linalg.solve_triangular(block, jnp.eye(NB, dtype=jnp.float32),...  25.3 us
    pallas_call x1, Pallas kernels, spread(): pl.pallas_call(functools.partial(spread_kernel, width, stride), out_shape...  20.3 us
    unnamed x39, local copies, waits for them, and re-layouts  18.6 us
  transfers between devices with their start and end apart: 16, of which 3 were waited for; matrix products, arithmetic and copies ran while one was open for 24% of the time, Pallas kernels for 15%

profile of v3, /device:TPU:7, one launch (start us, length us, event | category | flops | bytes accessed | tf_op | source)
XLA Modules:
  0.0 597.5 jit_solution(13899098377599453445)
XLA Ops:
  10.6 6.9 %shard_map.47 = f32[20,128,128]{2,1,0:T(8,128)S(1)} custom-call(s32[128]{0:T(128)S(1)} %get-tuple-element.269.slot_ref, s32[128]{0:T(128)} %valid_ref.1, f32[128,128,128]{2,1,0:T(8,128)} %tiles_ref.1), custom_call_target="tpu_custom_call" | custom-call | tf_op jit(solution)/shard_map/pallas_call | solution.py:56
  17.7 3.3 collective-permute-start.12
  24.8 20.3 %shard_map.46 = (f32[32,82,8,128]{3,2,1,0:T(8,128)S(1)}, s32[32,128]{1,0:T(8,128)S(1)}) custom-call(s32[6,128]{1,0:T(8,128)S(1)} %select_reduce_fusion.7.meta_ref, s32[2,16]{1,0:T(2,128)S(1)} %select_reduce_fusion.11.empty_ref, s32[3]{0:T(128)S(1)} %pad_add_fusion.1.count_ref, f32[128,16,8,128]{3,2,1,0:T(8,128)} %bitcast.182), custom_call_target="tpu_custom_call" | custom-call | tf_op jit(solution)/shard_map/pallas_call | solution.py:122
  45.1 4.2 copy-done.9
  49.4 3.0 shard_map.48
  54.5 11.7 %all_to_all.39 = s32[32,1,82]{2,1,0:T(1,128)S(1)} all-to-all(s32[32,1,82]{2,1,0:T(1,128)S(1)} %bitcast.181), channel_id=1, replica_groups=mesh['row'=4,'col'=8] {'row','col'}, dimensions={0} | all-to-all | bytes 20992 | tf_op jit(solution)/shard_map/all_to_all | solution.py:564
  66.2 6.0 %all-to-all-start.2 = ((f32[32,82,8,128]{3,2,1,0:T(8,128)}), f32[32,82,8,128]{3,2,1,0:T(8,128)}, u32[]{:S(2)}, u32[]{:S(2)}) async-start(f32[32,82,8,128]{3,2,1,0:T(8,128)} %copy-done.9), calls=%async_computation.3 | async-start | bytes 21495808 | tf_op jit(solution)/shard_map/all_to_all | solution.py:566
  72.2 5.6 copy.219
  77.9 120.5 %reduce-scatter.3.cloned.1.call-done = f32[512,256]{0,1:T(8,128)} async-done(((f32[4096,256]{0,1:T(8,128)}), f32[512,256]{0,1:T(8,128)}) %reduce-scatter.3.cloned.1.call-update) | async-done | bytes 524304 | tf_op jit(solution)/shard_map/reduce_scatter | solution.py:515
  206.5 6.1 %convert_reduce_fusion.1 = s32[2624]{0:T(1024)S(1)} fusion(s32[2624]{0:T(1024)S(1)} %get-tuple-element.268, s32[2624]{0:T(1024)S(1)} %get-tuple-element.267), kind=kLoop, calls=%fused_computation.99 | loop fusion | flops 34424256 | bytes 31488 | tf_op jit(solution)/shard_map/reduce_sum | solution.py:579
  218.5 35.1 %all-gather.8.cloned.1.call-done = f32[4096,256]{0,1:T(8,128)} async-done(((f32[512,256]{0,1:T(8,128)}), f32[4096,256]{0,1:T(8,128)}) %all-gather.8.cloned.1.call-update) | async-done | bytes 4194320 | tf_op jit(solution)/shard_map/all_gather | solution.py:516
  254.6 84.8 %all-to-all-done.2.arrived_ref = f32[32,82,8,128]{3,2,1,0:T(8,128)} async-done(((f32[32,82,8,128]{3,2,1,0:T(8,128)}), f32[32,82,8,128]{3,2,1,0:T(8,128)}, u32[]{:S(2)}, u32[]{:S(2)}) %all-to-all-start.2) | async-done | bytes 10747936 | tf_op jit(solution)/shard_map/all_to_all | solution.py:566
  339.5 11.2 %all-to-all-start.3 = ((s32[32,1,53]{2,1,0:T(1,128)}), s32[32,1,53]{2,1,0:T(1,128)S(1)}, u32[]{:S(2)}, u32[]{:S(2)}) async-start(s32[32,1,53]{2,1,0:T(1,128)} %bitcast.25), calls=%async_computation.4 | async-start | bytes 32768 | tf_op jit(solution)/shard_map/all_to_all | solution.py:594
  351.4 9.6 %shard_map.49 = f32[832,8,128]{2,1,0:T(8,128)} custom-call(s32[32,82]{1,0:T(8,128)S(1)} %add_select_fusion.13.slot_ref, f32[32,82,8,128]{3,2,1,0:T(8,128)} %all-to-all-done.2.arrived_ref), custom_call_target="tpu_custom_call" | custom-call | tf_op jit(solution)/shard_map/pallas_call | solution.py:155
  361.1 7.1 %all-to-all-start.4 = ((f32[16,52,8,128]{3,2,1,0:T(8,128)}), f32[16,52,8,128]{3,2,1,0:T(8,128)S(1)}, u32[]{:S(2)}, u32[]{:S(2)}) async-start(f32[16,52,8,128]{3,2,1,0:T(8,128)} %bitcast.47), calls=%async_computation.6 | async-start | bytes 6815744 | tf_op jit(solution)/shard_map/all_to_all | solution.py:641
  372.3 12.3 %custom-call.16 = f32[128,128]{1,0:T(8,128)} custom-call(f32[128,128]{1,0:T(8,128)S(1)} %copy.224), custom_call_target="Cholesky" | custom-call | tf_op jit(solution)/shard_map/jit(cholesky)/cholesky/custom-call.1 | solution.py:442
  389.2 10.4 %custom-call.17 = f32[1,128,128]{1,2,0:T(8,128)} custom-call(f32[1,128,128]{2,1,0:T(8,128)S(1)} %copy.227), custom_call_target="InvertDiagBlocksLowerTriangular" | custom-call | tf_op jit(solution)/shard_map/jit(_solve_triangular)/triangular_solve/custom-call.0 | solution.py:445
  412.7 13.2 %custom-call.18 = f32[128,128]{1,0:T(8,128)} custom-call(f32[128,128]{1,0:T(8,128)} %copy.234), custom_call_target="Cholesky" | custom-call | tf_op jit(solution)/shard_map/jit(cholesky)/cholesky/custom-call.1 | solution.py:442
  427.4 2.1 select_bitcast_fusion.2
  429.5 11.5 %custom-call.19 = f32[1,128,128]{1,2,0:T(8,128)} custom-call(f32[1,128,128]{2,1,0:T(8,128)} %get-tuple-element.221), custom_call_target="InvertDiagBlocksLowerTriangular" | custom-call | tf_op jit(solution)/shard_map/jit(_solve_triangular)/triangular_solve/custom-call.0 | solution.py:445
  445.1 3.6 reshape.1159
  448.7 4.6 collective-permute-start.15
  460.8 6.7 %constant_dynamic-slice_fusion.3 = (f32[1,512,256]{1,0,2:T(1,128)}, f32[1,512,256]{1,0,2:T(1,128)}, f32[1,512,256]{1,0,2:T(1,128)}, f32[1,512,256]{1,0,2:T(1,128)}) fusion(f32[4,512,256]{1,0,2:T(4,128)} %reshape.1159, s32[]{:T(128)S(6)} %select_n.694, s32[]{:T(128)S(6)} %select_n.700, s32[]{:T(128)S(6)} %select_n.698, s32[]{:T(128)S(6)} %select_n.696), kind=kLoop, calls=%fused_computation.294 | loop fusion | bytes 4194320 | tf_op jit(solution)/shard_map/jit(dynamic_index_in_dim)/dynamic_slice | solution.py:627
  478.3 4.5 collective-permute-start.19
  482.8 5.4 collective-permute-start.16
  489.5 6.0 %copy.236.raw_ref = f32[4096,256]{1,0:T(8,128)} copy(f32[4096,256]{0,1:T(8,128)} %all-gather.8.cloned.1.call-done) | data formatting | bytes 8388608 | tf_op jit(solution)/shard_map/optimization_barrier | solution.py:517
  502.6 2.2 copy-done.7
  505.7 5.1 shard_map.50
  510.8 2.6 copy-done.10
  517.0 3.6 shard_map.51
  523.7 49.9 %shard_map.52.partial_ref = f32[4096,2048]{1,0:T(8,128)} custom-call(s32[32,82]{1,0:T(8,128)} %get-tuple-element.261.code_ref, s32[32,82]{1,0:T(8,128)} %iota_subtract_fusion.run_ref, s32[2]{0:T(128)S(1)} %copy-done.32, f32[4096,2048]{1,0:T(8,128)} %front_ref.3, f32[4096,256]{1,0:T(8,128)} %copy-done.11, bf16[4096,768]{1,0:T(8,128)(2,1)} %copy-done.10, ...), custom_call_target="tpu_custom_call" | custom-call | tf_op jit(solution)/shard_map/pallas_call | solution.py:425
  578.1 11.6 %shard_map.53 = f32[4096,2048]{1,0:T(8,128)} custom-call(s32[832]{0:T(1024)S(1)} %get-tuple-element.184.block_ref, s32[832]{0:T(1024)S(1)} %get-tuple-element.183.unit_ref, s32[832]{0:T(1024)S(1)} %get-tuple-element.182.index_ref, s32[1]{0:T(128)} %bitcast.28.count_ref, f32[4096,2048]{1,0:T(8,128)} %shard_map.52.partial_ref, ...), custom_call_target="tpu_custom_call", output_to_operand_aliasing={{}: (4, {})} | custom-call | tf_op jit(solution)/shard_map/pallas_call | solution.py:234
  (187 shorter events, 90.1 us)
Async XLA Ops:
  8.0 9.6 %copy-start.31 = (s32[32,128]{1,0:T(8,128)}, s32[32,128]{1,0:T(8,128)S(1)}, u32[]{:S(2)}) copy-start(s32[32,128]{1,0:T(8,128)S(1)} %get-tuple-element.295) | copy-start | bytes 49156
  9.3 191.1 %copy-start.26 = (s32[32,128]{1,0:T(8,128)}, s32[32,128]{1,0:T(8,128)S(1)}, u32[]{:S(2)}) copy-start(s32[32,128]{1,0:T(8,128)S(1)} %convert_reduce_fusion.3) | copy-start | bytes 49156
  17.6 4.1 copy-start.27
  17.7 31.6 %collective-permute-start.12 = (f32[5,128,128]{2,1,0:T(8,128)S(1)}, f32[5,128,128]{2,1,0:T(8,128)S(1)}, u32[]{:S(2)}, u32[]{:S(2)}) collective-permute-start(f32[5,128,128]{2,1,0:T(8,128)S(1)} %get-tuple-element.250), channel_id=1, source_target_pairs={{0,24},{8,0},{16,8},{24,16},{1,25},{9,1},{17,9},{25,17},{2,26},{10... | collective-permute-start | bytes 983048 | tf_op jit(solution)/shard_map/ppermute | solution.py:502
  21.0 28.3 %collective-permute-start.11 = (f32[5,128,128]{2,1,0:T(8,128)S(1)}, f32[5,128,128]{2,1,0:T(8,128)S(1)}, u32[]{:S(2)}, u32[]{:S(2)}) collective-permute-start(f32[5,128,128]{2,1,0:T(8,128)S(1)} %get-tuple-element.251), channel_id=1, source_target_pairs={{0,16},{8,24},{16,0},{24,8},{1,17},{9,25},{17,1},{25,9},{2,18},{10... | collective-permute-start | bytes 983048 | tf_op jit(solution)/shard_map/ppermute | solution.py:502
  21.0 28.3 %collective-permute-start.10 = (f32[5,128,128]{2,1,0:T(8,128)S(1)}, f32[5,128,128]{2,1,0:T(8,128)S(1)}, u32[]{:S(2)}, u32[]{:S(2)}) collective-permute-start(f32[5,128,128]{2,1,0:T(8,128)S(1)} %get-tuple-element.252), channel_id=1, source_target_pairs={{0,8},{8,16},{16,24},{24,0},{1,9},{9,17},{17,25},{25,1},{2,10},{10... | collective-permute-start | bytes 983048 | tf_op jit(solution)/shard_map/ppermute | solution.py:502
  45.1 4.2 copy-start.9
  52.4 2.1 copy-start.8
  66.2 273.3 %all-to-all-start.2 = ((f32[32,82,8,128]{3,2,1,0:T(8,128)}), f32[32,82,8,128]{3,2,1,0:T(8,128)}, u32[]{:S(2)}, u32[]{:S(2)}) async-start(f32[32,82,8,128]{3,2,1,0:T(8,128)} %copy-done.9), calls=%async_computation.3 | async-start | bytes 21495808 | tf_op jit(solution)/shard_map/all_to_all | solution.py:566
  72.2 126.3 %reduce-scatter.3.cloned.1.call-start = ((), (), s32[]{:S(2)}) async-start(), calls=%async_computation.7 | async-start | bytes 4718592 | tf_op jit(solution)/shard_map/reduce_scatter | solution.py:515
  77.9 175.7 %all-gather.8.cloned.1.call-start = ((), (), s32[]{:S(2)}) async-start(), calls=%async_computation.8 | async-start | bytes 4718592 | tf_op jit(solution)/shard_map/all_gather | solution.py:516
  198.5 246.6 %all-gather.10.cloned.1.call-start = ((), (), s32[]{:S(2)}) async-start(), calls=%async_computation.9 | async-start | bytes 2621440 | tf_op jit(solution)/shard_map/all_gather | solution.py:518
  198.6 6.8 %copy-start.35 = (s32[128]{0:T(128)}, s32[128]{0:T(128)S(1)}, u32[]{:S(2)}) copy-start(s32[128]{0:T(128)S(1)} %iota_add_fusion.3) | copy-start | bytes 1540
  254.6 106.4 %copy-start.21 = (f32[256,256]{0,1:T(8,128)}, f32[256,256]{0,1:T(8,128)S(1)}, u32[]{:S(2)}) copy-start(f32[256,256]{0,1:T(8,128)S(1)} %convert_select_fusion.1) | copy-start | bytes 786436
  339.5 21.6 %all-to-all-start.3 = ((s32[32,1,53]{2,1,0:T(1,128)}), s32[32,1,53]{2,1,0:T(1,128)S(1)}, u32[]{:S(2)}, u32[]{:S(2)}) async-start(s32[32,1,53]{2,1,0:T(1,128)} %bitcast.25), calls=%async_computation.4 | async-start | bytes 32768 | tf_op jit(solution)/shard_map/all_to_all | solution.py:594
  361.1 7.2 %copy-start.36 = (s32[128]{0:T(128)S(1)}, s32[128]{0:T(128)}, u32[]{:S(2)}) copy-start(s32[128]{0:T(128)} %copy-done.35) | copy-start | bytes 1540
  361.1 217.0 %all-to-all-start.4 = ((f32[16,52,8,128]{3,2,1,0:T(8,128)}), f32[16,52,8,128]{3,2,1,0:T(8,128)S(1)}, u32[]{:S(2)}, u32[]{:S(2)}) async-start(f32[16,52,8,128]{3,2,1,0:T(8,128)} %bitcast.47), calls=%async_computation.6 | async-start | bytes 6815744 | tf_op jit(solution)/shard_map/all_to_all | solution.py:641
  445.1 10.2 %copy-start.30 = (pred[82,82]{1,0:T(8,128)(4,1)S(1)}, pred[82,82]{1,0:T(8,128)(4,1)}, u32[]{:S(2)}) copy-start(pred[82,82]{1,0:T(8,128)(4,1)} %iota_compare_fusion.24) | copy-start | bytes 20176
  445.1 10.2 %copy-start.34 = (pred[32,82]{1,0:T(8,128)(4,1)S(1)}, pred[32,82]{1,0:T(8,128)(4,1)}, u32[]{:S(2)}) copy-start(pred[32,82]{1,0:T(8,128)(4,1)} %get-tuple-element.225) | copy-start | bytes 7876
  448.7 29.6 %collective-permute-start.15 = (f32[256,256]{0,1:T(8,128)}, f32[256,256]{0,1:T(8,128)}, u32[]{:S(2)}, u32[]{:S(2)}) collective-permute-start(f32[256,256]{0,1:T(8,128)} %fusion.34), channel_id=1, source_target_pairs={{0,24},{1,25},{2,26},{3,27},{4,28},{5,29},{6,30},{7,31}} | collective-permute-start | bytes 786440 | tf_op jit(solution)/shard_map/ppermute | solution.py:632
  453.3 29.5 %collective-permute-start.14 = (f32[256,256]{0,1:T(8,128)}, f32[256,256]{0,1:T(8,128)}, u32[]{:S(2)}, u32[]{:S(2)}) collective-permute-start(f32[256,256]{0,1:T(8,128)} %fusion.34), channel_id=1, source_target_pairs={{0,16},{1,17},{2,18},{3,19},{4,20},{5,21},{6,22},{7,23}} | collective-permute-start | bytes 786440 | tf_op jit(solution)/shard_map/ppermute | solution.py:632
  458.9 39.9 %collective-permute-start.13 = (f32[256,256]{0,1:T(8,128)}, f32[256,256]{0,1:T(8,128)}, u32[]{:S(2)}, u32[]{:S(2)}) collective-permute-start(f32[256,256]{0,1:T(8,128)} %fusion.34), channel_id=1, source_target_pairs={{0,8},{1,9},{2,10},{3,11},{4,12},{5,13},{6,14},{7,15}} | collective-permute-start | bytes 786440 | tf_op jit(solution)/shard_map/ppermute | solution.py:632
  475.3 40.1 %collective-permute-start.17 = (f32[512,256]{1,0:T(8,128)}, f32[512,256]{1,0:T(8,128)}, u32[]{:S(2)}, u32[]{:S(2)}) collective-permute-start(f32[512,256]{1,0:T(8,128)} %bitcast.190), channel_id=1, source_target_pairs={{0,2},{1,4},{2,6},{3,0},{4,3},{5,5},{6,7},{7,1},{8,10},{9,12},{10,... | collective-permute-start | bytes 1572872 | tf_op jit(solution)/shard_map/ppermute | solution.py:628
  477.4 37.9 %collective-permute-start.18 = (f32[512,256]{1,0:T(8,128)}, f32[512,256]{1,0:T(8,128)}, u32[]{:S(2)}, u32[]{:S(2)}) collective-permute-start(f32[512,256]{1,0:T(8,128)} %bitcast.189), channel_id=1, source_target_pairs={{0,4},{1,6},{2,0},{3,2},{4,5},{5,7},{6,1},{7,3},{8,12},{9,14},{10,... | collective-permute-start | bytes 1572872 | tf_op jit(solution)/shard_map/ppermute | solution.py:628
  478.3 37.0 %collective-permute-start.19 = (f32[512,256]{1,0:T(8,128)}, f32[512,256]{1,0:T(8,128)}, u32[]{:S(2)}, u32[]{:S(2)}) collective-permute-start(f32[512,256]{1,0:T(8,128)} %bitcast.188), channel_id=1, source_target_pairs={{0,6},{1,0},{2,2},{3,4},{4,7},{5,1},{6,3},{7,5},{8,14},{9,8},{10,1... | collective-permute-start | bytes 1572872 | tf_op jit(solution)/shard_map/ppermute | solution.py:628
  482.8 32.5 %collective-permute-start.16 = (f32[512,256]{1,0:T(8,128)}, f32[512,256]{1,0:T(8,128)}, u32[]{:S(2)}, u32[]{:S(2)}) collective-permute-start(f32[512,256]{1,0:T(8,128)} %bitcast.187), channel_id=1, source_target_pairs={{0,0},{1,2},{2,4},{3,6},{4,1},{5,3},{6,5},{7,7},{8,8},{9,10},{10,1... | collective-permute-start | bytes 1572872 | tf_op jit(solution)/shard_map/ppermute | solution.py:628
  502.6 2.2 copy-start.7
  510.8 2.6 copy-start.10
  513.4 1.9 copy-start.11
  517.0 6.7 %copy-start.32 = (s32[2]{0:T(128)S(1)}, s32[2]{0:T(128)}, u32[]{:S(2)}) copy-start(s32[2]{0:T(128)} %pad_add_fusion.2.place_ref) | copy-start | bytes 28
  520.6 1.7 copy-start.12
  578.1 11.6 %copy-start.28 = (s32[128]{0:T(128)S(1)}, s32[128]{0:T(128)}, u32[]{:S(2)}) copy-start(s32[128]{0:T(128)} %valid_ref.1) | copy-start | bytes 1540
  (3 other events, 2.9 us)
Sparse Core Ops, SparseCore 0:
  78.0 120.4 reduce-scatter.2
  200.5 53.0 all-gather.7
  255.3 69.0 all-gather.9
